TPU v7x, 256 devices: a whole 4x4x8 slice. The times are simulated.
256 devices in a mesh: seg: 128 (over z, y, x), seq: 2 (over core).
Axes of the slice: x: 4, y: 4, z: 8, core: 2. Of those that a mesh axis runs over, the one named last changes fastest.
Arguments:
- latents: float32 [128, 256, 64], P('seg', 'seq'), may hold values from -6 to 6
- steps: int32 [128, 3], P('seg'), may hold values from 1 to 999, as said below
- text_hidden: bfloat16 [384, 2432], replicated, may hold values from -6 to 6
- text_len: int32 [1], replicated, may hold values from 192 to 384
- embed_in: bfloat16 [64, 2432], replicated, may hold values from -0.75 to 0.75
- time_proj: bfloat16 [256, 2432], replicated, may hold values from -0.375 to 0.375
- qkv_image: bfloat16 [2432, 3, 1536], P(None, None, 'seq'), may hold values from -0.125 to 0.125
- kv_text: bfloat16 [2432, 2, 1536], P(None, None, 'seq'), may hold values from -0.125 to 0.125
- out_proj: bfloat16 [1536, 2432], P('seq'), may hold values from -0.15625 to 0.15625
- embed_out: bfloat16 [2432, 64], replicated, may hold values from -0.125 to 0.125
Outputs:
- new_latents: float32 [128, 256, 64], P('seg', 'seq')
Inputs may be any that keep to these rules, and one draw needn't show every extreme that they name: `steps`: each row holds a start, a midpoint and an end timestep, strictly falling; a row's end is the next row's start; the first start is 999 and the last end is 1. Text slots from text_len on are padding.
All inputs are finite; a program needn't handle non-finite values.
Results may differ from a plain program's by a relative error of at most 0.0015.
Values may be sent and summed in bfloat16 or wider, within the bound.
No kernel may reach another device: no remote copies, remote signals or barrier semaphores. Data moves between devices by JAX's collectives and lax.ppermute only.
A program may use at most 128 MiB of HBM per device.

v0:
```python
import math

import jax
import jax.numpy as jnp
from jax import lax
from jax.sharding import PartitionSpec as P

HD = 64


epsilon = 1e-06


def prefix(value, axis, join, neutral):
    count, mine = (lax.axis_size(axis), lax.axis_index(axis))
    pieces = jax.tree.map(lambda part: lax.all_gather(part, axis), value)
    running = jax.tree.map(
        lambda part, zero: jnp.full_like(part, 0) + jnp.asarray(zero, part.dtype), value, neutral
    )

    def lap(position, running):
        longer = join(running, jax.tree.map(lambda part: part[position], pieces))
        return jax.tree.map(lambda new, old: jnp.where(position < mine, new, old), longer, running)

    return lax.fori_loop(0, count - 1, lap, running)


def layer_norm(hidden):
    average = jnp.mean(hidden, -1, keepdims=True)
    centred = hidden - average
    return centred * lax.rsqrt(jnp.mean(centred * centred, -1, keepdims=True) + epsilon)


def rms_heads(values, head_size):
    rows = values.shape[0]
    shaped = values.reshape(rows, -1, head_size)
    shaped = shaped * lax.rsqrt(jnp.mean(shaped * shaped, -1, keepdims=True) + epsilon)
    return shaped.reshape(rows, -1)


def time_embed(time_value, width):
    half_width = width // 2
    frequency = jnp.exp(-math.log(10000.0) * jnp.arange(half_width, dtype=jnp.float32) / half_width)
    angles = time_value * frequency
    return jnp.concatenate([jnp.cos(angles), jnp.sin(angles)])


def attend(queries, all_keys, all_values, live_mask, head_total, head_size):
    pieces = []
    for head_index in range(head_total):
        low = head_index * head_size
        high = low + head_size
        scores = jnp.einsum(
            "qd,kd->qk",
            queries[:, low:high],
            all_keys[:, low:high],
            preferred_element_type=jnp.float32,
        ) / math.sqrt(head_size)
        weight = jnp.exp(scores) * live_mask[None, :]
        totals = jnp.sum(weight, -1, keepdims=True)
        probability = (weight / totals).astype(jnp.bfloat16)
        pieces.append(
            jnp.dot(probability, all_values[:, low:high], preferred_element_type=jnp.float32)
        )
    return jnp.concatenate(pieces, 1).astype(jnp.bfloat16)


def combine(earlier, later):
    return (earlier[0] * later[0], later[0] * earlier[1] + later[1])


def per_device(
    latents,
    steps,
    text_hidden,
    text_len,
    embed_in,
    time_proj,
    qkv_image,
    kv_text,
    out_proj,
    embed_out,
):
    local_width = qkv_image.shape[2]
    local_heads = local_width // HD
    model_width = qkv_image.shape[0]
    qkv_flat = qkv_image.reshape(model_width, 3 * local_width)
    kv_flat = kv_text.reshape(model_width, 2 * local_width)
    text_slots = text_hidden.shape[0]
    live_text = (jnp.arange(text_slots) < text_len[0]).astype(jnp.float32)

    def velocity(latent, time_value):
        emb_vec = time_embed(time_value, time_proj.shape[0]).astype(jnp.bfloat16)
        time_vec = jnp.dot(emb_vec[None, :], time_proj, preferred_element_type=jnp.float32)
        hidden = (
            jnp.dot(latent.astype(jnp.bfloat16), embed_in, preferred_element_type=jnp.float32)
            + time_vec
        )
        normed = layer_norm(hidden).astype(jnp.bfloat16)
        projected = jnp.dot(
            lax.all_gather(normed, "seq", axis=0, tiled=True),
            qkv_flat,
            preferred_element_type=jnp.float32,
        )
        queries = rms_heads(projected[:, :local_width], HD).astype(jnp.bfloat16)
        key_img = rms_heads(projected[:, local_width : 2 * local_width], HD).astype(jnp.bfloat16)
        val_img = projected[:, 2 * local_width :].astype(jnp.bfloat16)
        text_norm = layer_norm(text_hidden.astype(jnp.float32) + time_vec).astype(jnp.bfloat16)
        text_proj = jnp.dot(text_norm, kv_flat, preferred_element_type=jnp.float32)
        key_txt = rms_heads(text_proj[:, :local_width], HD).astype(jnp.bfloat16)
        val_txt = text_proj[:, local_width:].astype(jnp.bfloat16)
        all_keys = jnp.concatenate([key_img, key_txt], 0)
        all_values = jnp.concatenate([val_img, val_txt], 0)
        live_mask = jnp.concatenate([jnp.ones((projected.shape[0],), jnp.float32), live_text])
        attended = attend(queries, all_keys, all_values, live_mask, local_heads, HD)
        mixed_out = lax.psum_scatter(
            jnp.dot(attended, out_proj, preferred_element_type=jnp.float32).astype(jnp.bfloat16),
            "seq",
            scatter_dimension=0,
            tiled=True,
        ).astype(jnp.float32)
        residual = hidden + mixed_out
        return jnp.dot(
            layer_norm(residual).astype(jnp.bfloat16), embed_out, preferred_element_type=jnp.float32
        )

    latent = latents[0]
    times = steps[0].astype(jnp.float32)
    sigma_start = times[0] / 1000.0
    sigma_mid = times[1] / 1000.0
    sigma_end = times[2] / 1000.0
    first_vel = velocity(latent, times[0])
    midpoint = latent + (sigma_mid - sigma_start) * first_vel
    second_vel = velocity(midpoint, times[1])
    fine_end = midpoint + (sigma_end - sigma_mid) * second_vel
    shrink = sigma_end / sigma_start
    segment = lax.axis_index("seg")
    shrink_arr = jnp.reshape(shrink, (1,))
    offset = jnp.where(segment == 0, fine_end, fine_end - shrink * latent)
    identity = (jnp.ones((1,), jnp.float32), jnp.zeros_like(offset))
    scanned = prefix((shrink_arr, offset), "seg", combine, identity)
    earlier = scanned[1]
    result = shrink * earlier + offset
    return result[None]


def solution(mesh):
    return jax.shard_map(
        per_device,
        mesh=mesh,
        in_specs=(
            P("seg", "seq", None),
            P("seg", None),
            P(),
            P(),
            P(),
            P(),
            P(None, None, "seq"),
            P(None, None, "seq"),
            P("seq", None),
            P(),
        ),
        out_specs=P("seg", "seq", None),
        check_vma=False,
    )
```

profile of v0, /device:TPU:0, one launch (start us, length us, event | category | flops | bytes accessed | tf_op | source)
XLA Modules:
  0.0 786.5 jit_solution(9395806565490099863)
XLA Ops:
  11.9 2.5 fusion.4
  15.8 4.4 copy.29
  20.3 6.3 fusion.15
  29.2 1.6 copy.18
  32.5 14.8 %copy.13 = bf16[2432,3,768]{0,2,1:T(8,128)(2,1)} copy(bf16[2432,3,768]{2,0,1:T(8,128)(2,1)} %param.18) | data formatting | bytes 22413312 | tf_op args[6]
  47.3 1.7 multiply_convert_fusion.5
  49.1 6.8 fusion.276
  63.4 2.0 multiply_convert_fusion.9
  75.3 4.3 convolution_convert_fusion.1
  81.0 13.9 %reduce-scatter.3.cloned.1.call-done = bf16[128,2432]{1,0:T(8,128)(2,1)} async-done(((bf16[256,2432]{1,0:T(8,128)(2,1)}), bf16[128,2432]{1,0:T(8,128)(2,1)}) %reduce-scatter.3.cloned.1.call-update) | async-done | bytes 622608 | tf_op jit(solution)/shard_map/reduce_scatter | solution.py:116
  100.2 5.6 fusion.13
  108.6 1.6 copy.24
  111.8 1.9 multiply_convert_fusion.4
  113.7 2.3 all-gather.7.cloned.1.call-done
  116.0 6.8 fusion.277
  129.0 1.8 multiply_convert_fusion.7
  142.6 4.3 convolution_convert_fusion
  147.7 14.3 %reduce-scatter.5.cloned.1.call-done = bf16[128,2432]{1,0:T(8,128)(2,1)} async-done(((bf16[256,2432]{1,0:T(8,128)(2,1)}), bf16[128,2432]{1,0:T(8,128)(2,1)}) %reduce-scatter.5.cloned.1.call-update) | async-done | bytes 622608 | tf_op jit(solution)/shard_map/reduce_scatter | solution.py:116
  166.9 350.4 %all-reduce.1 = f32[128]{0:T(128)S(1)} all-reduce(f32[128]{0:T(128)S(1)} %dynamic-update-slice), channel_id=1, replica_groups=mesh['seg'=128,'seq'=2] {'seg'}, use_global_device_ids=true, to_apply=%add.1 | all-reduce | flops 128 | bytes 1024
  517.3 7.0 copy.28
  524.3 254.9 %while.14 = (s32[]{:T(128)}, f32[128,64]{1,0:T(8,128)S(1)}, s32[]{:T(128)}, f32[128,1]{0,1:T(1,128)S(1)}, f32[128,128,64]{2,1,0:T(8,128)}, /*index=5*/s32[]{:T(128)}, s32[]{:T(128)}) while((s32[]{:T(128)}, f32[128,64]{1,0:T(8,128)S(1)}, s32[]{:T(128)}, f32[128,1]{0,1:T(1,128)S(1)}, f32[128,128,64]{2,1,0:T(8,128)}, ...), condition=%wide.region_45.46_spmd.clone, body=%wide.region_44.45_spmd.clone.sunk | while | flops 32772 | bytes 98429 | solution.py:25
  526.9 1.4 fusion.299
  532.9 1.4 fusion.299
  536.9 1.4 fusion.299
  541.0 1.4 fusion.299
  543.0 1.4 fusion.299
  547.0 1.4 fusion.299
  551.0 1.4 fusion.299
  557.0 1.4 fusion.299
  561.0 1.4 fusion.299
  565.0 1.4 fusion.299
  571.1 1.4 fusion.299
  (434 shorter events, 296.8 us)
Async XLA Ops:
  6.5 2.1 copy-start
  6.5 2.4 copy-start.20
  6.5 2.4 copy-start.12
  6.5 42.5 %all-gather.5.cloned.1.call-start = ((), (), s32[]{:S(2)}) async-start(), calls=%async_computation.2 | async-start | bytes 1867776 | tf_op jit(solution)/shard_map/all_gather | solution.py:101
  10.8 84.1 %reduce-scatter.3.cloned.1.call-start = ((), (), s32[]{:S(2)}) async-start(), calls=%async_computation.3 | async-start | bytes 1867776 | tf_op jit(solution)/shard_map/reduce_scatter | solution.py:116
  11.9 2.5 copy-start.3
  20.3 6.3 copy-start.2
  26.5 1.6 copy-start.9
  55.8 2.2 copy-start.8
  69.9 1.1 copy-start.16
  69.9 1.2 copy-start.19
  79.6 36.4 %all-gather.7.cloned.1.call-start = ((), (), s32[]{:S(2)}) async-start(), calls=%async_computation.4 | async-start | bytes 1867776 | tf_op jit(solution)/shard_map/all_gather | solution.py:101
  94.9 1.4 copy-start.6
  96.3 1.0 copy-start.14
  96.6 1.1 copy-start.13
  98.4 1.7 copy-start.4
  99.5 62.5 %reduce-scatter.5.cloned.1.call-start = ((), (), s32[]{:S(2)}) async-start(), calls=%async_computation.5 | async-start | bytes 1867776 | tf_op jit(solution)/shard_map/reduce_scatter | solution.py:116
  105.8 1.7 copy-start.10
  122.8 1.9 copy-start.7
  127.7 1.3 copy-start.11
  135.2 1.1 copy-start.17
  135.2 1.2 copy-start.18
  141.1 0.8 copy-start.22
  141.1 0.9 copy-start.23
  146.9 370.4 %all-gather.9.cloned.1.call-start = ((), (), s32[]{:S(2)}) async-start(), calls=%async_computation.6 | async-start | bytes 4227072 | tf_op jit(solution)/shard_map/all_gather | solution.py:16
  162.0 1.4 copy-start.5
  163.4 1.0 copy-start.15
  163.7 1.7 copy-start.24
  517.3 262.6 %copy-start.1 = (bf16[256,2432]{1,0:T(8,128)(2,1)S(1)}, bf16[256,2432]{1,0:T(8,128)(2,1)}, u32[]{:S(2)}) copy-start(bf16[256,2432]{1,0:T(8,128)(2,1)} %param.17) | copy-start | bytes 3735556
  524.3 255.0 %copy-start.21 = (f32[128,64]{0,1:T(8,128)S(1)}, f32[128,64]{0,1:T(8,128)}, u32[]{:S(2)}) copy-start(f32[128,64]{0,1:T(8,128)} %subtract_select_fusion) | copy-start | bytes 98308
Sparse Core Ops, SparseCore 0:
  10.9 16.1 all-gather.4
  79.8 15.0 reduce-scatter.2
  99.6 16.3 all-gather.6
  147.1 14.8 reduce-scatter.4
  165.5 117.4 all-gather.8
where the time goes:
time: 795 us; the launch traced here: 786 us
  blocking collectives  350 us (44%)
  other arithmetic  206 us (26%)
  local copies, waits for them, and re-layouts  124 us (16%)
  matrix products  55.3 us (7%)
  waiting for transfers between devices  30.7 us (4%)
  between operations  16.6 us (2%)
    unnamed x1, blocking collectives  350 us
    select_n x127, other arithmetic, lap(): jnp.where(position < mine, new, old)  181 us
    dynamic_slice x127, local copies, waits for them, and re-layouts, lap(): longer = join(running, jax.tree.map(lambda part: part[position], pieces))  70.8 us
    unnamed x56, local copies, waits for them, and re-layouts  32.4 us
    reduce_scatter x2, waiting for transfers between devices, velocity(): lax.psum_scatter(jnp.dot(attended, out_proj, preferred_element_type=jnp.f...  28.2 us
  transfers between devices with their start and end apart: 5, of which 3 were waited for; matrix products, arithmetic and copies ran while one was open for 7% of the time, Pallas kernels for 0%

commit v1 on v0

v1 whole, which is shorter than its diff:
```python
import math

import jax
import jax.numpy as jnp
import numpy as np
from jax import lax
from jax.experimental import pallas as pl
from jax.experimental.pallas import tpu as pltpu
from jax.sharding import PartitionSpec as P

HD = 64
CHUNK = 256
AUX = 16
epsilon = 1e-06
F32 = jnp.float32
BF16 = jnp.bfloat16


def dot(a, b):
    return jnp.dot(a, b, preferred_element_type=F32)


def dot_t(a, b):
    return lax.dot_general(a, b, (((1,), (1,)), ((), ())), preferred_element_type=F32)


def row_stats(x):
    mean = jnp.mean(x, -1, keepdims=True)
    centred = x - mean
    return mean, lax.rsqrt(jnp.mean(centred * centred, -1, keepdims=True) + epsilon)


def head_means():
    row = lax.broadcasted_iota(jnp.int32, (CHUNK, CHUNK), 0) // HD
    col = lax.broadcasted_iota(jnp.int32, (CHUNK, CHUNK), 1) // HD
    return jnp.where(row == col, 1.0 / HD, 0.0).astype(BF16)


def head_scale(y, means, scale):
    square = y * y
    high = square.astype(BF16)
    low = (square - high.astype(F32)).astype(BF16)
    mean = dot(high, means) + dot(low, means)
    return scale * lax.rsqrt(mean * (scale * scale) + epsilon)


def split(x):
    high = x.astype(BF16)
    return high, (x - high.astype(F32)).astype(BF16)


def time_rows(x, fifth=0.0):
    high, low = (part.astype(F32) for part in split(x))
    row = lax.broadcasted_iota(jnp.int32, (AUX, 1), 0)
    parts = (high[:1], low[:1], high[1:], low[1:], fifth)
    out = jnp.zeros((AUX, x.shape[1]), F32)
    for k, part in enumerate(parts):
        out = jnp.where(row == k, part, out)
    return out.astype(BF16)


def latent_rows(t, latent):
    z = latent.T.astype(BF16)
    col = lax.broadcasted_iota(jnp.int32, (z.shape[0], AUX), 1)
    pick = jnp.where(col // 2 == t, 1.0, 0.0).astype(BF16)
    return jnp.concatenate([z, z, pick], 1)


def prepare_kernel(
    steps, text_len, frequency, time_proj, embed_in, text, qkv, kv,
    mixed_embed, mixed_in, key0, key1, val0, val1,
    time_buf, embed_buf, text_rows, qkv_buf, kv_raw, kv_buf, embed_rows, stats, sems,
):
    parts = qkv.shape[2] // CHUNK
    slots, model = text.shape
    channels = embed_in.shape[0]
    copies = [
        pltpu.make_async_copy(time_proj, time_buf, sems.at[0]),
        pltpu.make_async_copy(embed_in, embed_buf, sems.at[1]),
        pltpu.make_async_copy(text, text_rows.at[pl.ds(0, slots)], sems.at[2]),
    ]
    steps_in = 3 * parts
    share = -(-model // steps_in // 16) * 16
    kv_rows = [(i * share, min(share, model - i * share)) for i in range(steps_in)]
    for i in range(steps_in):
        copies.append(
            pltpu.make_async_copy(
                qkv.at[i // parts, :, pl.ds(i % parts * CHUNK, CHUNK)], qkv_buf.at[i], sems.at[3 + i]
            )
        )
    kv_copies = []
    for i, (low, size) in enumerate(kv_rows):
        at = pl.ds(low, size)
        kv_copies.append(
            pltpu.make_async_copy(kv.at[at], kv_raw.at[at], sems.at[3 + steps_in + i])
        )
    for copy in copies[:2]:
        copy.start()
    for i in range(steps_in):
        kv_copies[i].start()
        copies[3 + i].start()
    copies[2].start()
    means = head_means()
    row = lax.broadcasted_iota(jnp.int32, (AUX, 1), 0)
    t0, t1 = steps[0, 0].astype(F32), steps[0, 1].astype(F32)
    angle = jnp.where(row % 2 == 0, t0, t1) * frequency[...]
    emb = jnp.concatenate([jnp.cos(angle), jnp.sin(angle)], 1).astype(BF16)
    copies[0].wait()
    time_vec = dot(emb, time_buf[...])
    high = time_vec.astype(BF16).astype(F32)
    aux = jnp.where(
        row < 2, high, jnp.where(row < 4, time_vec - high, jnp.where(row == 4, 1.0, 0.0))
    ).astype(BF16)
    time_mean = jnp.mean(time_vec[:2], -1, keepdims=True)
    time_centred = time_vec[:2] - time_mean
    of_times = jnp.mean(time_centred * time_centred, -1, keepdims=True)
    copies[1].wait()
    embed = embed_buf[...]
    embed_rows[:channels] = embed
    embed_rows[channels:] = aux
    embed_mean = jnp.mean(embed.astype(F32), -1, keepdims=True)

    def store_mixed(ref, at, of_embed, of_time):
        high, low = split(of_embed)
        ref[:channels, at] = high
        ref[channels : 2 * channels, at] = low
        ref[2 * channels :, at] = time_rows(of_time)

    store_mixed(mixed_embed, slice(None), embed.astype(F32) - embed_mean, time_centred)
    for i, (low, size) in enumerate(kv_rows):
        kv_copies[i].wait()
        copies[3 + i].wait()
        kv_buf[:, low : low + size] = jnp.swapaxes(kv_raw[low : low + size], 0, 1)
        at = slice(i * CHUNK, (i + 1) * CHUNK)
        out = dot(embed_rows[...], qkv_buf[i])
        ones = out[channels + 4 : channels + 5]
        of_time = out[channels : channels + 2] + out[channels + 2 : channels + 4]
        store_mixed(mixed_in, at, out[:channels] - embed_mean * ones, of_time - time_mean * ones)

    text_rows[slots:] = aux
    copies[2].wait()

    sums = dot_t(text_rows[:slots], time_rows(time_centred, 1.0))
    word_mean = sums[:, 4:5] * (1.0 / model)
    block = 48
    for i in range(slots // block):
        here = slice(i * block, (i + 1) * block)
        centred = text_rows[here].astype(F32) - word_mean[here]
        own = jnp.mean(centred * centred, -1, keepdims=True)
        for t in range(2):
            cross = (sums[here, 2 * t : 2 * t + 1] + sums[here, 2 * t + 1 : 2 * t + 2]) * (2.0 / model)
            scale = lax.rsqrt(own + cross + of_times[t : t + 1] + epsilon)
            stats[t, here] = jnp.broadcast_to(scale, (block, 128))

    live = lax.broadcasted_iota(jnp.int32, (slots, CHUNK), 0) < text_len[0]

    def text_project(i):
        return dot(text_rows[...], kv_buf[i // parts, :, i % parts * CHUNK : (i % parts + 1) * CHUNK])

    def text_store(i, out):
        at = slice(i % parts * CHUNK, (i % parts + 1) * CHUNK)
        ones = out[slots + 4 : slots + 5]
        base = out[:slots] - word_mean * ones
        for t in range(2):
            of_time = out[slots + t : slots + t + 1] + out[slots + 2 + t : slots + 3 + t]
            y = base + (of_time - time_mean[t : t + 1] * ones)
            scale = stats[t][:, :1]
            if i < parts:
                (key0, key1)[t][:, at] = (y * head_scale(y, means, scale)).astype(BF16)
            else:
                (val0, val1)[t][:, at] = jnp.where(live, y * scale, 0.0).astype(BF16)

    for i in range(2 * parts):
        text_store(i, text_project(i))


def attend(qkv, rows, text_len, text_key, text_val, store):
    width = text_key.shape[1]
    slots = text_key.shape[0]
    tokens = rows.stop - rows.start
    pair_width = 2 * HD
    first = lax.broadcasted_iota(jnp.int32, (tokens, pair_width), 1) < HD
    live = (lax.broadcasted_iota(jnp.int32, (slots, pair_width), 0) < text_len[0]).astype(BF16)
    always = jnp.ones((qkv.shape[0], pair_width), BF16)
    for pair in range(width // pair_width):
        at = slice(pair * pair_width, (pair + 1) * pair_width)
        q = qkv[rows, at]
        both = jnp.concatenate([jnp.where(first, q, 0), jnp.where(first, 0, q)], 0)
        image_key = qkv[:, width + at.start : width + at.stop]
        image_val = qkv[:, 2 * width + at.start : 2 * width + at.stop]
        p_image = jnp.exp2(dot_t(both, image_key)).astype(BF16)
        p_text = jnp.exp2(dot_t(both, text_key[:, at])).astype(BF16)
        out = dot(p_image, jnp.concatenate([image_val, always], 1)) + dot(
            p_text, jnp.concatenate([text_val[:, at], live], 1)
        )
        out = out[:, :pair_width] / out[:, pair_width:]
        store(at, jnp.where(first, out[:tokens], out[tokens:]).astype(BF16))


def theirs_kernel(
    t, text_len, mine, other, mixed_embed, mixed_in, text_key, text_val, qkv, out_other
):
    width = text_key.shape[1]
    tokens = mine.shape[1]
    rows = latent_rows(t, jnp.concatenate([mine[...], other[...]], 1))
    centred = dot(rows, mixed_embed[...])
    scale = lax.rsqrt(jnp.mean(centred * centred, -1, keepdims=True) + epsilon)
    means = head_means()
    for i in range(3 * width // CHUNK):
        at = slice(i * CHUNK, (i + 1) * CHUNK)
        y = dot(rows, mixed_in[:, at])
        if i < 2 * width // CHUNK:
            of_head = head_scale(y, means, scale)
            if i < width // CHUNK:
                of_head = of_head * (math.log2(math.e) / math.sqrt(HD))
            y = y * of_head
        else:
            y = y * scale
        qkv[:, at] = y.astype(BF16)

    def store(at, value):
        out_other[:, at] = value

    attend(qkv, slice(tokens, 2 * tokens), text_len, text_key, text_val, store)


def mine_kernel(
    t, text_len, qkv, mine, mixed_embed, text_key, text_val, proj_mine, residual, attended
):
    tokens = mine.shape[1]

    def store(at, value):
        attended[:, at] = value

    attend(qkv, slice(0, tokens), text_len, text_key, text_val, store)
    rows = latent_rows(t, mine[...])
    residual[...] = dot(rows, mixed_embed[...]) + dot(attended[...], proj_mine[...])


def output_kernel(t, steps, residual, came, latent, proj_other, embed_out, *rest):
    result = rest[-1]
    whole = residual[...] + dot(came[...], proj_other[...])
    mean, scale = row_stats(whole)
    normed = ((whole - mean) * scale).astype(BF16)
    velocity = dot_t(embed_out[...], normed)
    a, m, b = (steps[0, k].astype(F32) / 1000.0 for k in range(3))
    if t == 0:
        result[...] = latent[...] + (m - a) * velocity
    else:
        fine = latent[...] + (b - m) * velocity
        segment = lax.axis_index("seg")
        offset = jnp.where(segment == 0, fine, fine - b / a * rest[0][...])
        result[...] = offset / b


def prefix_sum(value, axis):
    count, mine = lax.axis_size(axis), lax.axis_index(axis)
    total = running = value
    base = 1
    while base < count:
        ways = 4 if count // base % 4 == 0 else 2
        place = mine // base % ways
        came = []
        for flip in (1, 3, 2)[: ways - 1]:
            pairs = []
            for s in range(count):
                partner = s ^ (flip * base)
                if ways == 2 and base > 1:
                    partner = s ^ (2 * base - base // 4)
                pairs.append((s, partner))
            came.append((flip, lax.ppermute(total, axis, pairs)))
        for flip, part in came:
            running = running + jnp.where((place ^ flip) < place, part, 0.0)
        for _, part in came:
            total = total + part
        base *= ways
    return running


VMEM = pl.BlockSpec(memory_space=pltpu.VMEM)
SMEM = pl.BlockSpec(memory_space=pltpu.SMEM)
ANY = pl.BlockSpec(memory_space=pl.ANY)


def per_device(
    latents, steps, text_hidden, text_len, embed_in, time_proj, qkv_image, kv_text, out_proj, embed_out
):
    model, _, width = qkv_image.shape
    slots = text_hidden.shape[0]
    channels = embed_in.shape[0]
    tokens = latents.shape[1]
    swap = [(0, 1), (1, 0)]
    half = time_proj.shape[0] // 2
    mixed = 2 * channels + AUX
    frequency = np.exp(-math.log(10000.0) * np.arange(half) / half).astype(np.float32)[None]
    latent = latents[0].T
    other = lax.ppermute(latent, "seq", swap)
    proj_other = lax.ppermute(out_proj, "seq", swap)
    embed_out_t = embed_out.T
    qkv_weights = jnp.transpose(qkv_image, (1, 0, 2))

    def call(kernel, name, outs, in_specs, scratch, limit, *args):
        return pl.pallas_call(
            kernel,
            out_shape=[pltpu.VMEM(dims, dtype) for dims, dtype in outs],
            in_specs=in_specs,
            out_specs=[VMEM] * len(outs),
            scratch_shapes=scratch,
            compiler_params=pltpu.CompilerParams(vmem_limit_bytes=limit << 20),
            name=name,
        )(*args)

    mixed_embed, mixed_in, key0, key1, val0, val1 = call(
        prepare_kernel,
        "prepare",
        [((mixed, model), BF16), ((mixed, 3 * width), BF16)] + [((slots, width), BF16)] * 4,
        [SMEM, SMEM, VMEM] + [ANY] * 5,
        [
            pltpu.VMEM(time_proj.shape, BF16),
            pltpu.VMEM(embed_in.shape, BF16),
            pltpu.VMEM((slots + AUX, model), BF16),
            pltpu.VMEM((3 * width // CHUNK, model, CHUNK), BF16),
            pltpu.VMEM(kv_text.shape, BF16),
            pltpu.VMEM((2, model, width), BF16),
            pltpu.VMEM((channels + AUX, model), BF16),
            pltpu.VMEM((2, slots, 128), F32),
            pltpu.SemaphoreType.DMA((3 + 6 * width // CHUNK,)),
        ],
        52,
        *(steps, text_len, frequency, time_proj, embed_in, text_hidden, qkv_weights, kv_text),
    )

    def evaluate(t, mine, other, text_key, text_val, *start):
        qkv, theirs = call(
            lambda *refs: theirs_kernel(t, *refs),
            "theirs",
            [((2 * tokens, 3 * width), BF16), ((tokens, width), BF16)],
            [SMEM] + [VMEM] * 6,
            [],
            16,
            *(text_len, mine, other, mixed_embed, mixed_in, text_key, text_val),
        )
        came = lax.ppermute(theirs, "seq", swap)
        (residual,) = call(
            lambda *refs: mine_kernel(t, *refs),
            "mine",
            [((tokens, model), F32)],
            [SMEM] + [VMEM] * 6,
            [pltpu.VMEM((tokens, width), BF16)],
            16,
            *(text_len, qkv, mine, mixed_embed, text_key, text_val, out_proj),
        )
        (result,) = call(
            lambda *refs: output_kernel(t, *refs),
            "output",
            [((channels, tokens), F32)],
            [SMEM] + [VMEM] * (5 + len(start)),
            [],
            16,
            *(steps, residual, came, mine, proj_other, embed_out_t, *start),
        )
        return result

    middle = evaluate(0, latent, other, key0, val0)
    offset = evaluate(1, middle, lax.ppermute(middle, "seq", swap), key1, val1, latent)
    result = steps[0, 2].astype(F32) / 1000.0 * prefix_sum(offset, "seg")
    return result.T[None]


def solution(mesh):
    return jax.shard_map(
        per_device,
        mesh=mesh,
        in_specs=(
            P("seg", "seq", None),
            P("seg", None),
            P(),
            P(),
            P(),
            P(),
            P(None, None, "seq"),
            P(None, None, "seq"),
            P("seq", None),
            P(),
        ),
        out_specs=P("seg", "seq", None),
        check_vma=False,
    )
```

time: 795 us -> 69.3 us (0.09)
  the two profiles are of different devices: /device:TPU:0 before, /device:TPU:32 now
where the time goes in v1:
time: 69.3 us; the launch traced here: 69.2 us
  Pallas kernels  31.3 us (45%)
  starting transfers between devices  18.8 us (27%)
  waiting for transfers between devices  16.3 us (24%)
  between operations  1.47 us (2%)
    pallas_call x7, Pallas kernels, call(): pl.pallas_call(kernel, out_shape=[pltpu.VMEM(dims, dtype) for dims, dtype...  31.3 us
    ppermute x10, starting transfers between devices, prefix_sum(): came.append((flip, lax.ppermute(total, axis, pairs)))  17.2 us
    ppermute x10, waiting for transfers between devices, prefix_sum(): came.append((flip, lax.ppermute(total, axis, pairs)))  15.4 us
  transfers between devices with their start and end apart: 15, of which 9 were waited for; matrix products, arithmetic and copies ran while one was open for 1% of the time, Pallas kernels for 35%

profile of v1, /device:TPU:32, one launch (start us, length us, event | category | flops | bytes accessed | tf_op | source)
XLA Modules:
  0.0 69.2 jit_solution(17798754767841879407)
XLA Ops:
  0.0 0.5 collective-permute-start
  1.2 16.5 %prepare.1 = (bf16[144,2432]{1,0:T(8,128)(2,1)S(1)}, bf16[144,2304]{1,0:T(8,128)(2,1)S(1)}, bf16[384,768]{1,0:T(8,128)(2,1)S(1)}, bf16[384,768]{1,0:T(8,128)(2,1...) custom-call(s32[1,3]{1,0:T(1,128)} %refs_0_.7, s32[1]{0:T(128)S(6)} %copy.12.text_len.refs_0_, ...), custom_call_target="tpu_custom_call" | custom-call | tf_op jit(solution)/shard_map/prepare/pallas_call | solution.py:303
  17.7 3.0 %theirs.2 = (bf16[256,2304]{1,0:T(8,128)(2,1)S(1)}, bf16[128,768]{1,0:T(8,128)(2,1)S(1)}) custom-call(s32[1]{0:T(128)S(6)} %copy.12.text_len.refs_0_, f32[64,128]{1,0:T(8,128)S(1)} %bitcast.13, f32[64,128]{1,0:T(8,128)S(1)} %collective-permute-done.refs_2_, bf16[144,2432]{1,0:T(8,128)(2,1)S(1)} %get-tuple-element.15.refs_3_, ...), custom_call_target="tpu_custom_call" | custom-call | tf_op jit(solution)/shard_map/theirs/pallas_call | solution.py:303
  20.7 0.1 collective-permute-start.1
  20.9 2.4 %mine.2.refs_1_ = f32[128,2432]{1,0:T(8,128)S(1)} custom-call(s32[1]{0:T(128)S(6)} %copy.12.text_len.refs_0_, bf16[256,2304]{1,0:T(8,128)(2,1)S(1)} %get-tuple-element.19.refs_1_, f32[64,128]{1,0:T(8,128)S(1)} %bitcast.14, bf16[144,2432]{1,0:T(8,128)(2,1)S(1)} %get-tuple-element.15.refs_3_, bf16[384,768]{1,0:T(8,128)(2,1)S(1)} %get-tuple-element.17.refs_5_.refs_4_, ...), custom_call_target="tpu_custom_call" | custom-call | tf_op jit(solution)/shard_map/mine/pallas_call | solution.py:303
  23.2 2.1 %output.2.refs_1_.refs_2_.refs_3_ = f32[64,128]{1,0:T(8,128)S(1)} custom-call(s32[1,3]{1,0:T(1,128)S(1)} %copy-done.3, f32[128,2432]{1,0:T(8,128)S(1)} %mine.2.refs_1_, bf16[128,768]{1,0:T(8,128)(2,1)S(1)} %collective-permute-done.1.refs_2_, f32[64,128]{1,0:T(8,128)S(1)} %bitcast.15, bf16[768,2432]{1,0:T(8,128)(2,1)S(1)} %collective-permute-done.2.refs_4_, ...), custom_call_target="tpu_custom_call" | custom-call | tf_op jit(solution)/shard_map/output/pallas_call | solution.py:303
  25.4 0.6 collective-permute-start.3
  25.9 0.9 %collective-permute-done.3.refs_2_ = f32[64,128]{1,0:T(8,128)S(1)} collective-permute-done((f32[64,128]{1,0:T(8,128)S(1)}, f32[64,128]{1,0:T(8,128)S(1)}, u32[]{:S(2)}, u32[]{:S(2)}) %collective-permute-start.3) | collective-permute-done | bytes 32800 | tf_op jit(solution)/shard_map/ppermute | solution.py:365
  26.8 2.8 %theirs.3 = (bf16[256,2304]{1,0:T(8,128)(2,1)S(1)}, bf16[128,768]{1,0:T(8,128)(2,1)S(1)}) custom-call(s32[1]{0:T(128)S(6)} %copy.12.text_len.refs_0_, f32[64,128]{1,0:T(8,128)S(1)} %output.2.refs_1_.refs_2_.refs_3_, f32[64,128]{1,0:T(8,128)S(1)} %collective-permute-done.3.refs_2_, bf16[144,2432]{1,0:T(8,128)(2,1)S(1)} %get-tuple-element.15.refs_3_, ...), custom_call_target="tpu_custom_call" | custom-call | tf_op jit(solution)/shard_map/theirs/pallas_call | solution.py:303
  29.6 0.4 collective-permute-start.4
  30.1 2.4 %mine.3.refs_1_ = f32[128,2432]{1,0:T(8,128)S(1)} custom-call(s32[1]{0:T(128)S(6)} %copy.12.text_len.refs_0_, bf16[256,2304]{1,0:T(8,128)(2,1)S(1)} %get-tuple-element.23.refs_1_, f32[64,128]{1,0:T(8,128)S(1)} %output.2.refs_1_.refs_2_.refs_3_, bf16[144,2432]{1,0:T(8,128)(2,1)S(1)} %get-tuple-element.15.refs_3_, ...), custom_call_target="tpu_custom_call" | custom-call | tf_op jit(solution)/shard_map/mine/pallas_call | solution.py:303
  32.4 2.1 %output.3 = f32[64,128]{1,0:T(8,128)S(1)} custom-call(s32[1,3]{1,0:T(1,128)S(1)} %copy-done.3, f32[128,2432]{1,0:T(8,128)S(1)} %mine.3.refs_1_, bf16[128,768]{1,0:T(8,128)(2,1)S(1)} %collective-permute-done.4.refs_2_, f32[64,128]{1,0:T(8,128)S(1)} %output.2.refs_1_.refs_2_.refs_3_, bf16[768,2432]{1,0:T(8,128)(2,1)S(1)} %collective-permute-done.2.refs_4_, ...), custom_call_target="tpu_custom_call" | custom-call | tf_op jit(solution)/shard_map/output/pallas_call | solution.py:303
  34.6 1.6 %collective-permute-start.5 = (f32[64,128]{1,0:T(8,128)S(1)}, f32[64,128]{1,0:T(8,128)S(1)}, u32[]{:S(2)}, u32[]{:S(2)}) collective-permute-start(f32[64,128]{1,0:T(8,128)S(1)} %output.3), channel_id=1, source_target_pairs={{0,2},{2,0},{4,6},{6,4},{8,10},{10,8},{12,14},{14,12},{16,18},{18,... | collective-permute-start | bytes 98312 | tf_op jit(solution)/shard_map/ppermute | solution.py:271
  36.2 2.1 %collective-permute-start.6 = (f32[64,128]{1,0:T(8,128)S(1)}, f32[64,128]{1,0:T(8,128)S(1)}, u32[]{:S(2)}, u32[]{:S(2)}) collective-permute-start(f32[64,128]{1,0:T(8,128)S(1)} %output.3), channel_id=1, source_target_pairs={{0,6},{2,4},{4,2},{6,0},{8,14},{10,12},{12,10},{14,8},{16,22},{18,... | collective-permute-start | bytes 98312 | tf_op jit(solution)/shard_map/ppermute | solution.py:271
  38.3 0.6 collective-permute-start.7
  38.9 2.4 %collective-permute-done.6 = f32[64,128]{1,0:T(8,128)S(1)} collective-permute-done((f32[64,128]{1,0:T(8,128)S(1)}, f32[64,128]{1,0:T(8,128)S(1)}, u32[]{:S(2)}, u32[]{:S(2)}) %collective-permute-start.6) | collective-permute-done | bytes 32800 | tf_op jit(solution)/shard_map/ppermute | solution.py:271
  41.3 2.4 %collective-permute-done.7 = f32[64,128]{1,0:T(8,128)S(1)} collective-permute-done((f32[64,128]{1,0:T(8,128)S(1)}, f32[64,128]{1,0:T(8,128)S(1)}, u32[]{:S(2)}, u32[]{:S(2)}) %collective-permute-start.7) | collective-permute-done | bytes 32800 | tf_op jit(solution)/shard_map/ppermute | solution.py:271
  43.7 3.3 %collective-permute-start.10 = (f32[64,128]{1,0:T(8,128)S(1)}, f32[64,128]{1,0:T(8,128)S(1)}, u32[]{:S(2)}, u32[]{:S(2)}) collective-permute-start(f32[64,128]{1,0:T(8,128)S(1)} %add_add_fusion.2), channel_id=1, source_target_pairs={{0,16},{2,18},{4,20},{6,22},{8,24},{10,26},{12,28},{14,30},{16,0},... | collective-permute-start | bytes 98312 | tf_op jit(solution)/shard_map/ppermute | solution.py:271
  47.0 0.7 collective-permute-start.8
  47.7 0.4 collective-permute-start.9
  48.0 1.2 %collective-permute-done.10 = f32[64,128]{1,0:T(8,128)S(1)} collective-permute-done((f32[64,128]{1,0:T(8,128)S(1)}, f32[64,128]{1,0:T(8,128)S(1)}, u32[]{:S(2)}, u32[]{:S(2)}) %collective-permute-start.10) | collective-permute-done | bytes 32800 | tf_op jit(solution)/shard_map/ppermute | solution.py:271
  49.2 1.7 %collective-permute-done.8 = f32[64,128]{1,0:T(8,128)S(1)} collective-permute-done((f32[64,128]{1,0:T(8,128)S(1)}, f32[64,128]{1,0:T(8,128)S(1)}, u32[]{:S(2)}, u32[]{:S(2)}) %collective-permute-start.8) | collective-permute-done | bytes 32800 | tf_op jit(solution)/shard_map/ppermute | solution.py:271
  50.9 1.9 %collective-permute-done.9 = f32[64,128]{1,0:T(8,128)S(1)} collective-permute-done((f32[64,128]{1,0:T(8,128)S(1)}, f32[64,128]{1,0:T(8,128)S(1)}, u32[]{:S(2)}, u32[]{:S(2)}) %collective-permute-start.9) | collective-permute-done | bytes 32800 | tf_op jit(solution)/shard_map/ppermute | solution.py:271
  52.8 0.2 collective-permute-start.11
  53.0 3.7 %collective-permute-start.12 = (f32[64,128]{1,0:T(8,128)S(1)}, f32[64,128]{1,0:T(8,128)S(1)}, u32[]{:S(2)}, u32[]{:S(2)}) collective-permute-start(f32[64,128]{1,0:T(8,128)S(1)} %add_add_fusion.1), channel_id=1, source_target_pairs={{0,96},{2,98},{4,100},{6,102},{8,104},{10,106},{12,108},{14,110},{... | collective-permute-start | bytes 98312 | tf_op jit(solution)/shard_map/ppermute | solution.py:271
  56.7 0.6 collective-permute-start.13
  57.3 1.3 %collective-permute-done.12 = f32[64,128]{1,0:T(8,128)S(1)} collective-permute-done((f32[64,128]{1,0:T(8,128)S(1)}, f32[64,128]{1,0:T(8,128)S(1)}, u32[]{:S(2)}, u32[]{:S(2)}) %collective-permute-start.12) | collective-permute-done | bytes 32800 | tf_op jit(solution)/shard_map/ppermute | solution.py:271
  58.6 2.9 %collective-permute-done.13 = f32[64,128]{1,0:T(8,128)S(1)} collective-permute-done((f32[64,128]{1,0:T(8,128)S(1)}, f32[64,128]{1,0:T(8,128)S(1)}, u32[]{:S(2)}, u32[]{:S(2)}) %collective-permute-start.13) | collective-permute-done | bytes 32800 | tf_op jit(solution)/shard_map/ppermute | solution.py:271
  61.5 4.1 %collective-permute-start.14 = (f32[64,128]{1,0:T(8,128)S(1)}, f32[64,128]{1,0:T(8,128)S(1)}, u32[]{:S(2)}, u32[]{:S(2)}) collective-permute-start(f32[64,128]{1,0:T(8,128)S(1)} %add_add_fusion), channel_id=1, source_target_pairs={{0,224},{2,226},{4,228},{6,230},{8,232},{10,234},{12,236},{14,238}... | collective-permute-start | bytes 98312 | tf_op jit(solution)/shard_map/ppermute | solution.py:271
  65.7 0.6 slice.3
  66.9 1.7 %collective-permute-done.14 = f32[64,128]{1,0:T(8,128)S(1)} collective-permute-done((f32[64,128]{1,0:T(8,128)S(1)}, f32[64,128]{1,0:T(8,128)S(1)}, u32[]{:S(2)}, u32[]{:S(2)}) %collective-permute-start.14) | collective-permute-done | bytes 32800 | tf_op jit(solution)/shard_map/ppermute | solution.py:271
  68.5 0.6 multiply_bitcast_fusion
  (18 shorter events, 0.1 us)
Async XLA Ops:
  0.0 23.2 %collective-permute-start.2 = (bf16[768,2432]{1,0:T(8,128)(2,1)}, bf16[768,2432]{1,0:T(8,128)(2,1)S(1)}, u32[]{:S(2)}, u32[]{:S(2)}) collective-permute-start(bf16[768,2432]{1,0:T(8,128)(2,1)} %refs_6_.3), channel_id=1, source_target_pairs={{0,1},{1,0},{2,3},{3,2},{4,5},{5,4},{6,7},{7,6},{8,9},{9,8},{10,11... | collective-permute-start | bytes 11206664 | tf_op jit(solution)/shard_map/ppermute | solution.py:298
  0.0 17.7 %collective-permute-start = (f32[64,128]{1,0:T(8,128)}, f32[64,128]{1,0:T(8,128)S(1)}, u32[]{:S(2)}, u32[]{:S(2)}) collective-permute-start(f32[64,128]{1,0:T(8,128)} %bitcast.12), channel_id=1, source_target_pairs={{0,1},{1,0},{2,3},{3,2},{4,5},{5,4},{6,7},{7,6},{8,9},{9,8},{10,11... | collective-permute-start | bytes 98312 | tf_op jit(solution)/shard_map/ppermute | solution.py:297
  1.2 16.5 %copy-start.2 = (f32[1,128,64]{1,2,0:T(8,128)S(1)}, f32[1,128,64]{1,2,0:T(8,128)}, u32[]{:S(2)}) copy-start(f32[1,128,64]{1,2,0:T(8,128)} %param.11) | copy-start | bytes 98308
  1.2 19.6 %copy-start = (bf16[768,2432]{1,0:T(8,128)(2,1)S(1)}, bf16[768,2432]{1,0:T(8,128)(2,1)}, u32[]{:S(2)}) copy-start(bf16[768,2432]{1,0:T(8,128)(2,1)} %refs_6_.3) | copy-start | bytes 11206660
  20.7 2.5 %collective-permute-start.1 = (bf16[128,768]{1,0:T(8,128)(2,1)S(1)}, bf16[128,768]{1,0:T(8,128)(2,1)S(1)}, u32[]{:S(2)}, u32[]{:S(2)}) collective-permute-start(bf16[128,768]{1,0:T(8,128)(2,1)S(1)} %get-tuple-element.20), channel_id=1, source_target_pairs={{0,1},{1,0},{2,3},{3,2},{4,5},{5,4},{6,7},{7,6},{8,9},{9,8},{10,11... | collective-permute-start | bytes 589832 | tf_op jit(solution)/shard_map/ppermute | solution.py:343
  20.8 2.4 %copy-start.1 = (bf16[2432,64]{0,1:T(8,128)(2,1)S(1)}, bf16[2432,64]{0,1:T(8,128)(2,1)}, u32[]{:S(2)}) copy-start(bf16[2432,64]{0,1:T(8,128)(2,1)} %param.20) | copy-start | bytes 933892
  20.8 2.4 %copy-start.3 = (s32[1,3]{1,0:T(1,128)S(1)}, s32[1,3]{1,0:T(1,128)}, u32[]{:S(2)}) copy-start(s32[1,3]{1,0:T(1,128)} %refs_0_.7) | copy-start | bytes 40
  25.4 1.4 %collective-permute-start.3 = (f32[64,128]{1,0:T(8,128)S(1)}, f32[64,128]{1,0:T(8,128)S(1)}, u32[]{:S(2)}, u32[]{:S(2)}) collective-permute-start(f32[64,128]{1,0:T(8,128)S(1)} %output.2.refs_1_.refs_2_.refs_3_), channel_id=1, source_target_pairs={{0,1},{1,0},{2,3},{3,2},{4,5},{5,4},{6,7},{7,6},{8,9},{9,8},{10,11... | collective-permute-start | bytes 98312 | tf_op jit(solution)/shard_map/ppermute | solution.py:365
  29.6 2.8 %collective-permute-start.4 = (bf16[128,768]{1,0:T(8,128)(2,1)S(1)}, bf16[128,768]{1,0:T(8,128)(2,1)S(1)}, u32[]{:S(2)}, u32[]{:S(2)}) collective-permute-start(bf16[128,768]{1,0:T(8,128)(2,1)S(1)} %get-tuple-element.24), channel_id=1, source_target_pairs={{0,1},{1,0},{2,3},{3,2},{4,5},{5,4},{6,7},{7,6},{8,9},{9,8},{10,11... | collective-permute-start | bytes 589832 | tf_op jit(solution)/shard_map/ppermute | solution.py:343
  34.6 4.3 %collective-permute-start.5 = (f32[64,128]{1,0:T(8,128)S(1)}, f32[64,128]{1,0:T(8,128)S(1)}, u32[]{:S(2)}, u32[]{:S(2)}) collective-permute-start(f32[64,128]{1,0:T(8,128)S(1)} %output.3), channel_id=1, source_target_pairs={{0,2},{2,0},{4,6},{6,4},{8,10},{10,8},{12,14},{14,12},{16,18},{18,... | collective-permute-start | bytes 98312 | tf_op jit(solution)/shard_map/ppermute | solution.py:271
  36.2 5.1 %collective-permute-start.6 = (f32[64,128]{1,0:T(8,128)S(1)}, f32[64,128]{1,0:T(8,128)S(1)}, u32[]{:S(2)}, u32[]{:S(2)}) collective-permute-start(f32[64,128]{1,0:T(8,128)S(1)} %output.3), channel_id=1, source_target_pairs={{0,6},{2,4},{4,2},{6,0},{8,14},{10,12},{12,10},{14,8},{16,22},{18,... | collective-permute-start | bytes 98312 | tf_op jit(solution)/shard_map/ppermute | solution.py:271
  38.3 5.4 %collective-permute-start.7 = (f32[64,128]{1,0:T(8,128)S(1)}, f32[64,128]{1,0:T(8,128)S(1)}, u32[]{:S(2)}, u32[]{:S(2)}) collective-permute-start(f32[64,128]{1,0:T(8,128)S(1)} %output.3), channel_id=1, source_target_pairs={{0,4},{2,6},{4,0},{6,2},{8,12},{10,14},{12,8},{14,10},{16,20},{18,... | collective-permute-start | bytes 98312 | tf_op jit(solution)/shard_map/ppermute | solution.py:271
  43.7 5.5 %collective-permute-start.10 = (f32[64,128]{1,0:T(8,128)S(1)}, f32[64,128]{1,0:T(8,128)S(1)}, u32[]{:S(2)}, u32[]{:S(2)}) collective-permute-start(f32[64,128]{1,0:T(8,128)S(1)} %add_add_fusion.2), channel_id=1, source_target_pairs={{0,16},{2,18},{4,20},{6,22},{8,24},{10,26},{12,28},{14,30},{16,0},... | collective-permute-start | bytes 98312 | tf_op jit(solution)/shard_map/ppermute | solution.py:271
  47.0 3.9 %collective-permute-start.8 = (f32[64,128]{1,0:T(8,128)S(1)}, f32[64,128]{1,0:T(8,128)S(1)}, u32[]{:S(2)}, u32[]{:S(2)}) collective-permute-start(f32[64,128]{1,0:T(8,128)S(1)} %add_add_fusion.2), channel_id=1, source_target_pairs={{0,8},{2,10},{4,12},{6,14},{8,0},{10,2},{12,4},{14,6},{16,24},{18,... | collective-permute-start | bytes 98312 | tf_op jit(solution)/shard_map/ppermute | solution.py:271
  47.7 5.1 %collective-permute-start.9 = (f32[64,128]{1,0:T(8,128)S(1)}, f32[64,128]{1,0:T(8,128)S(1)}, u32[]{:S(2)}, u32[]{:S(2)}) collective-permute-start(f32[64,128]{1,0:T(8,128)S(1)} %add_add_fusion.2), channel_id=1, source_target_pairs={{0,24},{2,26},{4,28},{6,30},{8,16},{10,18},{12,20},{14,22},{16,8},... | collective-permute-start | bytes 98312 | tf_op jit(solution)/shard_map/ppermute | solution.py:271
  52.8 4.5 %collective-permute-start.11 = (f32[64,128]{1,0:T(8,128)S(1)}, f32[64,128]{1,0:T(8,128)S(1)}, u32[]{:S(2)}, u32[]{:S(2)}) collective-permute-start(f32[64,128]{1,0:T(8,128)S(1)} %add_add_fusion.1), channel_id=1, source_target_pairs={{0,32},{2,34},{4,36},{6,38},{8,40},{10,42},{12,44},{14,46},{16,48}... | collective-permute-start | bytes 98312 | tf_op jit(solution)/shard_map/ppermute | solution.py:271
  53.0 5.6 %collective-permute-start.12 = (f32[64,128]{1,0:T(8,128)S(1)}, f32[64,128]{1,0:T(8,128)S(1)}, u32[]{:S(2)}, u32[]{:S(2)}) collective-permute-start(f32[64,128]{1,0:T(8,128)S(1)} %add_add_fusion.1), channel_id=1, source_target_pairs={{0,96},{2,98},{4,100},{6,102},{8,104},{10,106},{12,108},{14,110},{... | collective-permute-start | bytes 98312 | tf_op jit(solution)/shard_map/ppermute | solution.py:271
  56.7 4.8 %collective-permute-start.13 = (f32[64,128]{1,0:T(8,128)S(1)}, f32[64,128]{1,0:T(8,128)S(1)}, u32[]{:S(2)}, u32[]{:S(2)}) collective-permute-start(f32[64,128]{1,0:T(8,128)S(1)} %add_add_fusion.1), channel_id=1, source_target_pairs={{0,64},{2,66},{4,68},{6,70},{8,72},{10,74},{12,76},{14,78},{16,80}... | collective-permute-start | bytes 98312 | tf_op jit(solution)/shard_map/ppermute | solution.py:271
  61.5 7.0 %collective-permute-start.14 = (f32[64,128]{1,0:T(8,128)S(1)}, f32[64,128]{1,0:T(8,128)S(1)}, u32[]{:S(2)}, u32[]{:S(2)}) collective-permute-start(f32[64,128]{1,0:T(8,128)S(1)} %add_add_fusion), channel_id=1, source_target_pairs={{0,224},{2,226},{4,228},{6,230},{8,232},{10,234},{12,236},{14,238}... | collective-permute-start | bytes 98312 | tf_op jit(solution)/shard_map/ppermute | solution.py:271

commit v2 on v1

--- a/solution.py
+++ b/solution.py
@@ -74,38 +74,33 @@
     parts = qkv.shape[2] // CHUNK
     slots, model = text.shape
     channels = embed_in.shape[0]
-    copies = [
+    small = [
         pltpu.make_async_copy(time_proj, time_buf, sems.at[0]),
         pltpu.make_async_copy(embed_in, embed_buf, sems.at[1]),
         pltpu.make_async_copy(text, text_rows.at[pl.ds(0, slots)], sems.at[2]),
     ]
-    steps_in = 3 * parts
-    share = -(-model // steps_in // 16) * 16
-    kv_rows = [(i * share, min(share, model - i * share)) for i in range(steps_in)]
-    for i in range(steps_in):
-        copies.append(
-            pltpu.make_async_copy(
-                qkv.at[i // parts, :, pl.ds(i % parts * CHUNK, CHUNK)], qkv_buf.at[i], sems.at[3 + i]
-            )
-        )
+    kv_rows = [(low, min(CHUNK, model - low)) for low in range(0, model, CHUNK)]
     kv_copies = []
     for i, (low, size) in enumerate(kv_rows):
         at = pl.ds(low, size)
-        kv_copies.append(
-            pltpu.make_async_copy(kv.at[at], kv_raw.at[at], sems.at[3 + steps_in + i])
+        kv_copies.append(pltpu.make_async_copy(kv.at[at], kv_raw.at[at], sems.at[3 + i]))
+    qkv_copies = []
+    for i in range(3 * parts):
+        qkv_copies.append(
+            pltpu.make_async_copy(
+                qkv.at[i // parts, :, pl.ds(i % parts * CHUNK, CHUNK)],
+                qkv_buf.at[i],
+                sems.at[3 + len(kv_rows) + i],
+            )
         )
-    for copy in copies[:2]:
+    for copy in small + kv_copies + qkv_copies:
         copy.start()
-    for i in range(steps_in):
-        kv_copies[i].start()
-        copies[3 + i].start()
-    copies[2].start()
     means = head_means()
     row = lax.broadcasted_iota(jnp.int32, (AUX, 1), 0)
     t0, t1 = steps[0, 0].astype(F32), steps[0, 1].astype(F32)
     angle = jnp.where(row % 2 == 0, t0, t1) * frequency[...]
     emb = jnp.concatenate([jnp.cos(angle), jnp.sin(angle)], 1).astype(BF16)
-    copies[0].wait()
+    small[0].wait()
     time_vec = dot(emb, time_buf[...])
     high = time_vec.astype(BF16).astype(F32)
     aux = jnp.where(
@@ -114,11 +109,6 @@
     time_mean = jnp.mean(time_vec[:2], -1, keepdims=True)
     time_centred = time_vec[:2] - time_mean
     of_times = jnp.mean(time_centred * time_centred, -1, keepdims=True)
-    copies[1].wait()
-    embed = embed_buf[...]
-    embed_rows[:channels] = embed
-    embed_rows[channels:] = aux
-    embed_mean = jnp.mean(embed.astype(F32), -1, keepdims=True)
 
     def store_mixed(ref, at, of_embed, of_time):
         high, low = split(of_embed)
@@ -126,20 +116,15 @@
         ref[channels : 2 * channels, at] = low
         ref[2 * channels :, at] = time_rows(of_time)
 
+    small[1].wait()
+    embed = embed_buf[...]
+    embed_rows[:channels] = embed
+    embed_rows[channels:] = aux
+    embed_mean = jnp.mean(embed.astype(F32), -1, keepdims=True)
     store_mixed(mixed_embed, slice(None), embed.astype(F32) - embed_mean, time_centred)
-    for i, (low, size) in enumerate(kv_rows):
-        kv_copies[i].wait()
-        copies[3 + i].wait()
-        kv_buf[:, low : low + size] = jnp.swapaxes(kv_raw[low : low + size], 0, 1)
-        at = slice(i * CHUNK, (i + 1) * CHUNK)
-        out = dot(embed_rows[...], qkv_buf[i])
-        ones = out[channels + 4 : channels + 5]
-        of_time = out[channels : channels + 2] + out[channels + 2 : channels + 4]
-        store_mixed(mixed_in, at, out[:channels] - embed_mean * ones, of_time - time_mean * ones)
 
     text_rows[slots:] = aux
-    copies[2].wait()
-
+    small[2].wait()
     sums = dot_t(text_rows[:slots], time_rows(time_centred, 1.0))
     word_mean = sums[:, 4:5] * (1.0 / model)
     block = 48
@@ -170,8 +155,26 @@
             else:
                 (val0, val1)[t][:, at] = jnp.where(live, y * scale, 0.0).astype(BF16)
 
+    def image_chunk(i):
+        at = slice(i * CHUNK, (i + 1) * CHUNK)
+        out = dot(embed_rows[...], qkv_buf[i])
+        ones = out[channels + 4 : channels + 5]
+        of_time = out[channels : channels + 2] + out[channels + 2 : channels + 4]
+        store_mixed(mixed_in, at, out[:channels] - embed_mean * ones, of_time - time_mean * ones)
+
+    for copy in kv_copies:
+        copy.wait()
+    for low, size in kv_rows:
+        kv_buf[:, low : low + size] = jnp.swapaxes(kv_raw[low : low + size], 0, 1)
+    out = text_project(0)
     for i in range(2 * parts):
-        text_store(i, text_project(i))
+        later = text_project(i + 1) if i + 1 < 2 * parts else None
+        text_store(i, out)
+        out = later
+    for copy in qkv_copies:
+        copy.wait()
+    for i in range(3 * parts):
+        image_chunk(i)
 
 
 def attend(qkv, rows, text_len, text_key, text_val, store):
@@ -182,19 +185,28 @@
     first = lax.broadcasted_iota(jnp.int32, (tokens, pair_width), 1) < HD
     live = (lax.broadcasted_iota(jnp.int32, (slots, pair_width), 0) < text_len[0]).astype(BF16)
     always = jnp.ones((qkv.shape[0], pair_width), BF16)
-    for pair in range(width // pair_width):
+    pairs = width // pair_width
+
+    def scores(pair):
         at = slice(pair * pair_width, (pair + 1) * pair_width)
         q = qkv[rows, at]
         both = jnp.concatenate([jnp.where(first, q, 0), jnp.where(first, 0, q)], 0)
         image_key = qkv[:, width + at.start : width + at.stop]
+        return dot_t(both, image_key), dot_t(both, text_key[:, at])
+
+    of_image, of_text = scores(0)
+    for pair in range(pairs):
+        later = scores(pair + 1) if pair + 1 < pairs else (None, None)
+        at = slice(pair * pair_width, (pair + 1) * pair_width)
         image_val = qkv[:, 2 * width + at.start : 2 * width + at.stop]
-        p_image = jnp.exp2(dot_t(both, image_key)).astype(BF16)
-        p_text = jnp.exp2(dot_t(both, text_key[:, at])).astype(BF16)
+        p_image = jnp.exp2(of_image).astype(BF16)
+        p_text = jnp.exp2(of_text).astype(BF16)
         out = dot(p_image, jnp.concatenate([image_val, always], 1)) + dot(
             p_text, jnp.concatenate([text_val[:, at], live], 1)
         )
         out = out[:, :pair_width] / out[:, pair_width:]
         store(at, jnp.where(first, out[:tokens], out[tokens:]).astype(BF16))
+        of_image, of_text = later
 
 
 def theirs_kernel(
@@ -206,9 +218,13 @@
     centred = dot(rows, mixed_embed[...])
     scale = lax.rsqrt(jnp.mean(centred * centred, -1, keepdims=True) + epsilon)
     means = head_means()
-    for i in range(3 * width // CHUNK):
+    chunks = 3 * width // CHUNK
+    out = dot(rows, mixed_in[:, :CHUNK])
+    for i in range(chunks):
         at = slice(i * CHUNK, (i + 1) * CHUNK)
-        y = dot(rows, mixed_in[:, at])
+        y = out
+        if i + 1 < chunks:
+            out = dot(rows, mixed_in[:, (i + 1) * CHUNK : (i + 2) * CHUNK])
         if i < 2 * width // CHUNK:
             of_head = head_scale(y, means, scale)
             if i < width // CHUNK:
@@ -324,7 +340,7 @@
             pltpu.VMEM((2, model, width), BF16),
             pltpu.VMEM((channels + AUX, model), BF16),
             pltpu.VMEM((2, slots, 128), F32),
-            pltpu.SemaphoreType.DMA((3 + 6 * width // CHUNK,)),
+            pltpu.SemaphoreType.DMA((3 + 3 * width // CHUNK + -(-model // CHUNK),)),
         ],
         52,
         *(steps, text_len, frequency, time_proj, embed_in, text_hidden, qkv_weights, kv_text),

time: 69.3 us -> 65.7 us (0.948)
  Pallas kernels: 31.3 us -> 27.5 us
    pallas_call x7, Pallas kernels: 31.3 us -> 27.5 us  [call(): pl.pallas_call(kernel, out_shape=[pltpu.VMEM(dims, dtype) for dims, dtype...]
  transfers between devices with their start and end apart: 15 -> 15, of which waited for: 9 -> 9; matrix products, arithmetic and copies ran while one was open for 1% -> 1% of each run, Pallas kernels for 35% -> 31%
where the time goes in v2:
time: 65.7 us; the launch traced here: 65.6 us
  Pallas kernels  27.5 us (42%)
  starting transfers between devices  19 us (29%)
  waiting for transfers between devices  16.3 us (25%)
  between operations  1.47 us (2%)
  other arithmetic  0.68 us (1%)
    pallas_call x7, Pallas kernels, call(): pl.pallas_call(kernel, out_shape=[pltpu.VMEM(dims, dtype) for dims, dtype...  27.5 us
    ppermute x10, starting transfers between devices, prefix_sum(): came.append((flip, lax.ppermute(total, axis, pairs)))  17.3 us
    ppermute x10, waiting for transfers between devices, prefix_sum(): came.append((flip, lax.ppermute(total, axis, pairs)))  15.4 us
  transfers between devices with their start and end apart: 15, of which 9 were waited for; matrix products, arithmetic and copies ran while one was open for 1% of the time, Pallas kernels for 31%

profile of v2, /device:TPU:32, one launch (start us, length us, event | category | flops | bytes accessed | tf_op | source)
XLA Modules:
  0.0 65.6 jit_solution(2384838934170734609)
XLA Ops:
  0.0 0.5 collective-permute-start
  1.2 13.7 %prepare.1 = (bf16[144,2432]{1,0:T(8,128)(2,1)S(1)}, bf16[144,2304]{1,0:T(8,128)(2,1)S(1)}, bf16[384,768]{1,0:T(8,128)(2,1)S(1)}, bf16[384,768]{1,0:T(8,128)(2,1...) custom-call(s32[1,3]{1,0:T(1,128)} %refs_0_.7, s32[1]{0:T(128)S(6)} %copy.12.text_len.refs_0_, ...), custom_call_target="tpu_custom_call" | custom-call | tf_op jit(solution)/shard_map/prepare/pallas_call | solution.py:319
  14.9 2.7 %theirs.2 = (bf16[256,2304]{1,0:T(8,128)(2,1)S(1)}, bf16[128,768]{1,0:T(8,128)(2,1)S(1)}) custom-call(s32[1]{0:T(128)S(6)} %copy.12.text_len.refs_0_, f32[64,128]{1,0:T(8,128)S(1)} %bitcast.13, f32[64,128]{1,0:T(8,128)S(1)} %collective-permute-done.refs_2_, bf16[144,2432]{1,0:T(8,128)(2,1)S(1)} %get-tuple-element.15.refs_3_, ...), custom_call_target="tpu_custom_call" | custom-call | tf_op jit(solution)/shard_map/theirs/pallas_call | solution.py:319
  17.6 0.3 collective-permute-start.1
  17.9 2.1 %mine.2.refs_1_ = f32[128,2432]{1,0:T(8,128)S(1)} custom-call(s32[1]{0:T(128)S(6)} %copy.12.text_len.refs_0_, bf16[256,2304]{1,0:T(8,128)(2,1)S(1)} %get-tuple-element.19.refs_1_, f32[64,128]{1,0:T(8,128)S(1)} %bitcast.14, bf16[144,2432]{1,0:T(8,128)(2,1)S(1)} %get-tuple-element.15.refs_3_, bf16[384,768]{1,0:T(8,128)(2,1)S(1)} %get-tuple-element.17.refs_5_.refs_4_, ...), custom_call_target="tpu_custom_call" | custom-call | tf_op jit(solution)/shard_map/mine/pallas_call | solution.py:319
  20.1 2.1 %output.2.refs_1_.refs_2_.refs_3_ = f32[64,128]{1,0:T(8,128)S(1)} custom-call(s32[1,3]{1,0:T(1,128)S(1)} %copy-done.3, f32[128,2432]{1,0:T(8,128)S(1)} %mine.2.refs_1_, bf16[128,768]{1,0:T(8,128)(2,1)S(1)} %collective-permute-done.1.refs_2_, f32[64,128]{1,0:T(8,128)S(1)} %bitcast.15, bf16[768,2432]{1,0:T(8,128)(2,1)S(1)} %collective-permute-done.2.refs_4_, ...), custom_call_target="tpu_custom_call" | custom-call | tf_op jit(solution)/shard_map/output/pallas_call | solution.py:319
  22.2 0.5 collective-permute-start.3
  22.7 0.9 %collective-permute-done.3.refs_2_ = f32[64,128]{1,0:T(8,128)S(1)} collective-permute-done((f32[64,128]{1,0:T(8,128)S(1)}, f32[64,128]{1,0:T(8,128)S(1)}, u32[]{:S(2)}, u32[]{:S(2)}) %collective-permute-start.3) | collective-permute-done | bytes 32800 | tf_op jit(solution)/shard_map/ppermute | solution.py:381
  23.6 2.7 %theirs.3 = (bf16[256,2304]{1,0:T(8,128)(2,1)S(1)}, bf16[128,768]{1,0:T(8,128)(2,1)S(1)}) custom-call(s32[1]{0:T(128)S(6)} %copy.12.text_len.refs_0_, f32[64,128]{1,0:T(8,128)S(1)} %output.2.refs_1_.refs_2_.refs_3_, f32[64,128]{1,0:T(8,128)S(1)} %collective-permute-done.3.refs_2_, bf16[144,2432]{1,0:T(8,128)(2,1)S(1)} %get-tuple-element.15.refs_3_, ...), custom_call_target="tpu_custom_call" | custom-call | tf_op jit(solution)/shard_map/theirs/pallas_call | solution.py:319
  26.3 0.4 collective-permute-start.4
  26.7 2.1 %mine.3.refs_1_ = f32[128,2432]{1,0:T(8,128)S(1)} custom-call(s32[1]{0:T(128)S(6)} %copy.12.text_len.refs_0_, bf16[256,2304]{1,0:T(8,128)(2,1)S(1)} %get-tuple-element.23.refs_1_, f32[64,128]{1,0:T(8,128)S(1)} %output.2.refs_1_.refs_2_.refs_3_, bf16[144,2432]{1,0:T(8,128)(2,1)S(1)} %get-tuple-element.15.refs_3_, ...), custom_call_target="tpu_custom_call" | custom-call | tf_op jit(solution)/shard_map/mine/pallas_call | solution.py:319
  28.8 2.1 %output.3 = f32[64,128]{1,0:T(8,128)S(1)} custom-call(s32[1,3]{1,0:T(1,128)S(1)} %copy-done.3, f32[128,2432]{1,0:T(8,128)S(1)} %mine.3.refs_1_, bf16[128,768]{1,0:T(8,128)(2,1)S(1)} %collective-permute-done.4.refs_2_, f32[64,128]{1,0:T(8,128)S(1)} %output.2.refs_1_.refs_2_.refs_3_, bf16[768,2432]{1,0:T(8,128)(2,1)S(1)} %collective-permute-done.2.refs_4_, ...), custom_call_target="tpu_custom_call" | custom-call | tf_op jit(solution)/shard_map/output/pallas_call | solution.py:319
  31.0 1.6 %collective-permute-start.5 = (f32[64,128]{1,0:T(8,128)S(1)}, f32[64,128]{1,0:T(8,128)S(1)}, u32[]{:S(2)}, u32[]{:S(2)}) collective-permute-start(f32[64,128]{1,0:T(8,128)S(1)} %output.3), channel_id=1, source_target_pairs={{0,2},{2,0},{4,6},{6,4},{8,10},{10,8},{12,14},{14,12},{16,18},{18,... | collective-permute-start | bytes 98312 | tf_op jit(solution)/shard_map/ppermute | solution.py:287
  32.5 2.1 %collective-permute-start.6 = (f32[64,128]{1,0:T(8,128)S(1)}, f32[64,128]{1,0:T(8,128)S(1)}, u32[]{:S(2)}, u32[]{:S(2)}) collective-permute-start(f32[64,128]{1,0:T(8,128)S(1)} %output.3), channel_id=1, source_target_pairs={{0,6},{2,4},{4,2},{6,0},{8,14},{10,12},{12,10},{14,8},{16,22},{18,... | collective-permute-start | bytes 98312 | tf_op jit(solution)/shard_map/ppermute | solution.py:287
  34.6 0.6 collective-permute-start.7
  35.3 2.4 %collective-permute-done.6 = f32[64,128]{1,0:T(8,128)S(1)} collective-permute-done((f32[64,128]{1,0:T(8,128)S(1)}, f32[64,128]{1,0:T(8,128)S(1)}, u32[]{:S(2)}, u32[]{:S(2)}) %collective-permute-start.6) | collective-permute-done | bytes 32800 | tf_op jit(solution)/shard_map/ppermute | solution.py:287
  37.7 2.4 %collective-permute-done.7 = f32[64,128]{1,0:T(8,128)S(1)} collective-permute-done((f32[64,128]{1,0:T(8,128)S(1)}, f32[64,128]{1,0:T(8,128)S(1)}, u32[]{:S(2)}, u32[]{:S(2)}) %collective-permute-start.7) | collective-permute-done | bytes 32800 | tf_op jit(solution)/shard_map/ppermute | solution.py:287
  40.1 3.3 %collective-permute-start.10 = (f32[64,128]{1,0:T(8,128)S(1)}, f32[64,128]{1,0:T(8,128)S(1)}, u32[]{:S(2)}, u32[]{:S(2)}) collective-permute-start(f32[64,128]{1,0:T(8,128)S(1)} %add_add_fusion.2), channel_id=1, source_target_pairs={{0,16},{2,18},{4,20},{6,22},{8,24},{10,26},{12,28},{14,30},{16,0},... | collective-permute-start | bytes 98312 | tf_op jit(solution)/shard_map/ppermute | solution.py:287
  43.4 0.7 %collective-permute-start.8 = (f32[64,128]{1,0:T(8,128)S(1)}, f32[64,128]{1,0:T(8,128)S(1)}, u32[]{:S(2)}, u32[]{:S(2)}) collective-permute-start(f32[64,128]{1,0:T(8,128)S(1)} %add_add_fusion.2), channel_id=1, source_target_pairs={{0,8},{2,10},{4,12},{6,14},{8,0},{10,2},{12,4},{14,6},{16,24},{18,... | collective-permute-start | bytes 98312 | tf_op jit(solution)/shard_map/ppermute | solution.py:287
  44.0 0.4 collective-permute-start.9
  44.4 1.2 %collective-permute-done.10 = f32[64,128]{1,0:T(8,128)S(1)} collective-permute-done((f32[64,128]{1,0:T(8,128)S(1)}, f32[64,128]{1,0:T(8,128)S(1)}, u32[]{:S(2)}, u32[]{:S(2)}) %collective-permute-start.10) | collective-permute-done | bytes 32800 | tf_op jit(solution)/shard_map/ppermute | solution.py:287
  45.6 1.7 %collective-permute-done.8 = f32[64,128]{1,0:T(8,128)S(1)} collective-permute-done((f32[64,128]{1,0:T(8,128)S(1)}, f32[64,128]{1,0:T(8,128)S(1)}, u32[]{:S(2)}, u32[]{:S(2)}) %collective-permute-start.8) | collective-permute-done | bytes 32800 | tf_op jit(solution)/shard_map/ppermute | solution.py:287
  47.3 1.9 %collective-permute-done.9 = f32[64,128]{1,0:T(8,128)S(1)} collective-permute-done((f32[64,128]{1,0:T(8,128)S(1)}, f32[64,128]{1,0:T(8,128)S(1)}, u32[]{:S(2)}, u32[]{:S(2)}) %collective-permute-start.9) | collective-permute-done | bytes 32800 | tf_op jit(solution)/shard_map/ppermute | solution.py:287
  49.2 0.2 collective-permute-start.11
  49.4 3.7 %collective-permute-start.12 = (f32[64,128]{1,0:T(8,128)S(1)}, f32[64,128]{1,0:T(8,128)S(1)}, u32[]{:S(2)}, u32[]{:S(2)}) collective-permute-start(f32[64,128]{1,0:T(8,128)S(1)} %add_add_fusion.1), channel_id=1, source_target_pairs={{0,96},{2,98},{4,100},{6,102},{8,104},{10,106},{12,108},{14,110},{... | collective-permute-start | bytes 98312 | tf_op jit(solution)/shard_map/ppermute | solution.py:287
  53.1 0.6 collective-permute-start.13
  53.7 1.3 %collective-permute-done.12 = f32[64,128]{1,0:T(8,128)S(1)} collective-permute-done((f32[64,128]{1,0:T(8,128)S(1)}, f32[64,128]{1,0:T(8,128)S(1)}, u32[]{:S(2)}, u32[]{:S(2)}) %collective-permute-start.12) | collective-permute-done | bytes 32800 | tf_op jit(solution)/shard_map/ppermute | solution.py:287
  55.0 2.9 %collective-permute-done.13 = f32[64,128]{1,0:T(8,128)S(1)} collective-permute-done((f32[64,128]{1,0:T(8,128)S(1)}, f32[64,128]{1,0:T(8,128)S(1)}, u32[]{:S(2)}, u32[]{:S(2)}) %collective-permute-start.13) | collective-permute-done | bytes 32800 | tf_op jit(solution)/shard_map/ppermute | solution.py:287
  57.9 4.1 %collective-permute-start.14 = (f32[64,128]{1,0:T(8,128)S(1)}, f32[64,128]{1,0:T(8,128)S(1)}, u32[]{:S(2)}, u32[]{:S(2)}) collective-permute-start(f32[64,128]{1,0:T(8,128)S(1)} %add_add_fusion), channel_id=1, source_target_pairs={{0,224},{2,226},{4,228},{6,230},{8,232},{10,234},{12,236},{14,238}... | collective-permute-start | bytes 98312 | tf_op jit(solution)/shard_map/ppermute | solution.py:287
  62.0 0.6 slice.3
  63.3 1.6 %collective-permute-done.14 = f32[64,128]{1,0:T(8,128)S(1)} collective-permute-done((f32[64,128]{1,0:T(8,128)S(1)}, f32[64,128]{1,0:T(8,128)S(1)}, u32[]{:S(2)}, u32[]{:S(2)}) %collective-permute-start.14) | collective-permute-done | bytes 32800 | tf_op jit(solution)/shard_map/ppermute | solution.py:287
  64.9 0.6 multiply_bitcast_fusion
  (18 shorter events, 0.1 us)
Async XLA Ops:
  0.0 20.0 %collective-permute-start.2 = (bf16[768,2432]{1,0:T(8,128)(2,1)}, bf16[768,2432]{1,0:T(8,128)(2,1)S(1)}, u32[]{:S(2)}, u32[]{:S(2)}) collective-permute-start(bf16[768,2432]{1,0:T(8,128)(2,1)} %refs_6_.3), channel_id=1, source_target_pairs={{0,1},{1,0},{2,3},{3,2},{4,5},{5,4},{6,7},{7,6},{8,9},{9,8},{10,11... | collective-permute-start | bytes 11206664 | tf_op jit(solution)/shard_map/ppermute | solution.py:314
  0.0 14.9 %collective-permute-start = (f32[64,128]{1,0:T(8,128)}, f32[64,128]{1,0:T(8,128)S(1)}, u32[]{:S(2)}, u32[]{:S(2)}) collective-permute-start(f32[64,128]{1,0:T(8,128)} %bitcast.12), channel_id=1, source_target_pairs={{0,1},{1,0},{2,3},{3,2},{4,5},{5,4},{6,7},{7,6},{8,9},{9,8},{10,11... | collective-permute-start | bytes 98312 | tf_op jit(solution)/shard_map/ppermute | solution.py:313
  1.2 13.7 %copy-start.2 = (f32[1,128,64]{1,2,0:T(8,128)S(1)}, f32[1,128,64]{1,2,0:T(8,128)}, u32[]{:S(2)}) copy-start(f32[1,128,64]{1,2,0:T(8,128)} %param.11) | copy-start | bytes 98308
  1.2 16.7 %copy-start = (bf16[768,2432]{1,0:T(8,128)(2,1)S(1)}, bf16[768,2432]{1,0:T(8,128)(2,1)}, u32[]{:S(2)}) copy-start(bf16[768,2432]{1,0:T(8,128)(2,1)} %refs_6_.3) | copy-start | bytes 11206660
  17.6 2.4 %collective-permute-start.1 = (bf16[128,768]{1,0:T(8,128)(2,1)S(1)}, bf16[128,768]{1,0:T(8,128)(2,1)S(1)}, u32[]{:S(2)}, u32[]{:S(2)}) collective-permute-start(bf16[128,768]{1,0:T(8,128)(2,1)S(1)} %get-tuple-element.20), channel_id=1, source_target_pairs={{0,1},{1,0},{2,3},{3,2},{4,5},{5,4},{6,7},{7,6},{8,9},{9,8},{10,11... | collective-permute-start | bytes 589832 | tf_op jit(solution)/shard_map/ppermute | solution.py:359
  17.9 2.1 %copy-start.1 = (bf16[2432,64]{0,1:T(8,128)(2,1)S(1)}, bf16[2432,64]{0,1:T(8,128)(2,1)}, u32[]{:S(2)}) copy-start(bf16[2432,64]{0,1:T(8,128)(2,1)} %param.20) | copy-start | bytes 933892
  17.9 2.1 %copy-start.3 = (s32[1,3]{1,0:T(1,128)S(1)}, s32[1,3]{1,0:T(1,128)}, u32[]{:S(2)}) copy-start(s32[1,3]{1,0:T(1,128)} %refs_0_.7) | copy-start | bytes 40
  22.2 1.4 %collective-permute-start.3 = (f32[64,128]{1,0:T(8,128)S(1)}, f32[64,128]{1,0:T(8,128)S(1)}, u32[]{:S(2)}, u32[]{:S(2)}) collective-permute-start(f32[64,128]{1,0:T(8,128)S(1)} %output.2.refs_1_.refs_2_.refs_3_), channel_id=1, source_target_pairs={{0,1},{1,0},{2,3},{3,2},{4,5},{5,4},{6,7},{7,6},{8,9},{9,8},{10,11... | collective-permute-start | bytes 98312 | tf_op jit(solution)/shard_map/ppermute | solution.py:381
  26.3 2.5 %collective-permute-start.4 = (bf16[128,768]{1,0:T(8,128)(2,1)S(1)}, bf16[128,768]{1,0:T(8,128)(2,1)S(1)}, u32[]{:S(2)}, u32[]{:S(2)}) collective-permute-start(bf16[128,768]{1,0:T(8,128)(2,1)S(1)} %get-tuple-element.24), channel_id=1, source_target_pairs={{0,1},{1,0},{2,3},{3,2},{4,5},{5,4},{6,7},{7,6},{8,9},{9,8},{10,11... | collective-permute-start | bytes 589832 | tf_op jit(solution)/shard_map/ppermute | solution.py:359
  31.0 4.3 %collective-permute-start.5 = (f32[64,128]{1,0:T(8,128)S(1)}, f32[64,128]{1,0:T(8,128)S(1)}, u32[]{:S(2)}, u32[]{:S(2)}) collective-permute-start(f32[64,128]{1,0:T(8,128)S(1)} %output.3), channel_id=1, source_target_pairs={{0,2},{2,0},{4,6},{6,4},{8,10},{10,8},{12,14},{14,12},{16,18},{18,... | collective-permute-start | bytes 98312 | tf_op jit(solution)/shard_map/ppermute | solution.py:287
  32.5 5.1 %collective-permute-start.6 = (f32[64,128]{1,0:T(8,128)S(1)}, f32[64,128]{1,0:T(8,128)S(1)}, u32[]{:S(2)}, u32[]{:S(2)}) collective-permute-start(f32[64,128]{1,0:T(8,128)S(1)} %output.3), channel_id=1, source_target_pairs={{0,6},{2,4},{4,2},{6,0},{8,14},{10,12},{12,10},{14,8},{16,22},{18,... | collective-permute-start | bytes 98312 | tf_op jit(solution)/shard_map/ppermute | solution.py:287
  34.6 5.4 %collective-permute-start.7 = (f32[64,128]{1,0:T(8,128)S(1)}, f32[64,128]{1,0:T(8,128)S(1)}, u32[]{:S(2)}, u32[]{:S(2)}) collective-permute-start(f32[64,128]{1,0:T(8,128)S(1)} %output.3), channel_id=1, source_target_pairs={{0,4},{2,6},{4,0},{6,2},{8,12},{10,14},{12,8},{14,10},{16,20},{18,... | collective-permute-start | bytes 98312 | tf_op jit(solution)/shard_map/ppermute | solution.py:287
  40.1 5.5 %collective-permute-start.10 = (f32[64,128]{1,0:T(8,128)S(1)}, f32[64,128]{1,0:T(8,128)S(1)}, u32[]{:S(2)}, u32[]{:S(2)}) collective-permute-start(f32[64,128]{1,0:T(8,128)S(1)} %add_add_fusion.2), channel_id=1, source_target_pairs={{0,16},{2,18},{4,20},{6,22},{8,24},{10,26},{12,28},{14,30},{16,0},... | collective-permute-start | bytes 98312 | tf_op jit(solution)/shard_map/ppermute | solution.py:287
  43.4 3.9 %collective-permute-start.8 = (f32[64,128]{1,0:T(8,128)S(1)}, f32[64,128]{1,0:T(8,128)S(1)}, u32[]{:S(2)}, u32[]{:S(2)}) collective-permute-start(f32[64,128]{1,0:T(8,128)S(1)} %add_add_fusion.2), channel_id=1, source_target_pairs={{0,8},{2,10},{4,12},{6,14},{8,0},{10,2},{12,4},{14,6},{16,24},{18,... | collective-permute-start | bytes 98312 | tf_op jit(solution)/shard_map/ppermute | solution.py:287
  44.0 5.1 %collective-permute-start.9 = (f32[64,128]{1,0:T(8,128)S(1)}, f32[64,128]{1,0:T(8,128)S(1)}, u32[]{:S(2)}, u32[]{:S(2)}) collective-permute-start(f32[64,128]{1,0:T(8,128)S(1)} %add_add_fusion.2), channel_id=1, source_target_pairs={{0,24},{2,26},{4,28},{6,30},{8,16},{10,18},{12,20},{14,22},{16,8},... | collective-permute-start | bytes 98312 | tf_op jit(solution)/shard_map/ppermute | solution.py:287
  49.2 4.5 %collective-permute-start.11 = (f32[64,128]{1,0:T(8,128)S(1)}, f32[64,128]{1,0:T(8,128)S(1)}, u32[]{:S(2)}, u32[]{:S(2)}) collective-permute-start(f32[64,128]{1,0:T(8,128)S(1)} %add_add_fusion.1), channel_id=1, source_target_pairs={{0,32},{2,34},{4,36},{6,38},{8,40},{10,42},{12,44},{14,46},{16,48}... | collective-permute-start | bytes 98312 | tf_op jit(solution)/shard_map/ppermute | solution.py:287
  49.4 5.6 %collective-permute-start.12 = (f32[64,128]{1,0:T(8,128)S(1)}, f32[64,128]{1,0:T(8,128)S(1)}, u32[]{:S(2)}, u32[]{:S(2)}) collective-permute-start(f32[64,128]{1,0:T(8,128)S(1)} %add_add_fusion.1), channel_id=1, source_target_pairs={{0,96},{2,98},{4,100},{6,102},{8,104},{10,106},{12,108},{14,110},{... | collective-permute-start | bytes 98312 | tf_op jit(solution)/shard_map/ppermute | solution.py:287
  53.1 4.8 %collective-permute-start.13 = (f32[64,128]{1,0:T(8,128)S(1)}, f32[64,128]{1,0:T(8,128)S(1)}, u32[]{:S(2)}, u32[]{:S(2)}) collective-permute-start(f32[64,128]{1,0:T(8,128)S(1)} %add_add_fusion.1), channel_id=1, source_target_pairs={{0,64},{2,66},{4,68},{6,70},{8,72},{10,74},{12,76},{14,78},{16,80}... | collective-permute-start | bytes 98312 | tf_op jit(solution)/shard_map/ppermute | solution.py:287
  57.9 7.0 %collective-permute-start.14 = (f32[64,128]{1,0:T(8,128)S(1)}, f32[64,128]{1,0:T(8,128)S(1)}, u32[]{:S(2)}, u32[]{:S(2)}) collective-permute-start(f32[64,128]{1,0:T(8,128)S(1)} %add_add_fusion), channel_id=1, source_target_pairs={{0,224},{2,226},{4,228},{6,230},{8,232},{10,234},{12,236},{14,238}... | collective-permute-start | bytes 98312 | tf_op jit(solution)/shard_map/ppermute | solution.py:287

commit v3 on v2

--- a/solution.py
+++ b/solution.py
@@ -277,7 +277,7 @@
         ways = 4 if count // base % 4 == 0 else 2
         place = mine // base % ways
         came = []
-        for flip in (1, 3, 2)[: ways - 1]:
+        for flip in (2, 3, 1)[4 - ways :]:
             pairs = []
             for s in range(count):
                 partner = s ^ (flip * base)

time: 65.7 us -> 64.4 us (0.980)
  waiting for transfers between devices: 16.3 us -> 12.8 us
  starting transfers between devices: 19 us -> 21.1 us
    ppermute x10, waiting for transfers between devices: 15.4 us -> 11.9 us  [prefix_sum(): came.append((flip, lax.ppermute(total, axis, pairs)))]
    ppermute x10, starting transfers between devices: 17.3 us -> 19.3 us  [prefix_sum(): came.append((flip, lax.ppermute(total, axis, pairs)))]
  transfers between devices with their start and end apart: 15 -> 15, of which waited for: 9 -> 8; matrix products, arithmetic and copies ran while one was open for 1% -> 1% of each run, Pallas kernels for 31% -> 32%
where the time goes in v3:
time: 64.4 us; the launch traced here: 64.1 us
  Pallas kernels  27.5 us (43%)
  starting transfers between devices  21.1 us (33%)
  waiting for transfers between devices  12.8 us (20%)
  between operations  1.47 us (2%)
  other arithmetic  0.68 us (1%)
    pallas_call x7, Pallas kernels, call(): pl.pallas_call(kernel, out_shape=[pltpu.VMEM(dims, dtype) for dims, dtype...  27.5 us
    ppermute x10, starting transfers between devices, prefix_sum(): came.append((flip, lax.ppermute(total, axis, pairs)))  19.3 us
    ppermute x10, waiting for transfers between devices, prefix_sum(): came.append((flip, lax.ppermute(total, axis, pairs)))  11.9 us
  transfers between devices with their start and end apart: 15, of which 8 were waited for; matrix products, arithmetic and copies ran while one was open for 1% of the time, Pallas kernels for 32%

profile of v3, /device:TPU:32, one launch (start us, length us, event | category | flops | bytes accessed | tf_op | source)
XLA Modules:
  0.0 64.1 jit_solution(2024846165728611897)
XLA Ops:
  0.0 0.0 collective-permute-start.2
  0.0 0.5 collective-permute-start
  1.2 13.7 %prepare.1 = (bf16[144,2432]{1,0:T(8,128)(2,1)S(1)}, bf16[144,2304]{1,0:T(8,128)(2,1)S(1)}, bf16[384,768]{1,0:T(8,128)(2,1)S(1)}, bf16[384,768]{1,0:T(8,128)(2,1...) custom-call(s32[1,3]{1,0:T(1,128)} %refs_0_.7, s32[1]{0:T(128)S(6)} %copy.12.text_len.refs_0_, ...), custom_call_target="tpu_custom_call" | custom-call | tf_op jit(solution)/shard_map/prepare/pallas_call | solution.py:319
  14.9 2.7 %theirs.2 = (bf16[256,2304]{1,0:T(8,128)(2,1)S(1)}, bf16[128,768]{1,0:T(8,128)(2,1)S(1)}) custom-call(s32[1]{0:T(128)S(6)} %copy.12.text_len.refs_0_, f32[64,128]{1,0:T(8,128)S(1)} %bitcast.13, f32[64,128]{1,0:T(8,128)S(1)} %collective-permute-done.refs_2_, bf16[144,2432]{1,0:T(8,128)(2,1)S(1)} %get-tuple-element.15.refs_3_, ...), custom_call_target="tpu_custom_call" | custom-call | tf_op jit(solution)/shard_map/theirs/pallas_call | solution.py:319
  17.6 0.3 collective-permute-start.1
  17.9 0.0 copy-start.1
  17.9 0.0 copy-start.3
  17.9 2.1 %mine.2.refs_1_ = f32[128,2432]{1,0:T(8,128)S(1)} custom-call(s32[1]{0:T(128)S(6)} %copy.12.text_len.refs_0_, bf16[256,2304]{1,0:T(8,128)(2,1)S(1)} %get-tuple-element.19.refs_1_, f32[64,128]{1,0:T(8,128)S(1)} %bitcast.14, bf16[144,2432]{1,0:T(8,128)(2,1)S(1)} %get-tuple-element.15.refs_3_, bf16[384,768]{1,0:T(8,128)(2,1)S(1)} %get-tuple-element.17.refs_5_.refs_4_, ...), custom_call_target="tpu_custom_call" | custom-call | tf_op jit(solution)/shard_map/mine/pallas_call | solution.py:319
  20.1 2.1 %output.2.refs_1_.refs_2_.refs_3_ = f32[64,128]{1,0:T(8,128)S(1)} custom-call(s32[1,3]{1,0:T(1,128)S(1)} %copy-done.3, f32[128,2432]{1,0:T(8,128)S(1)} %mine.2.refs_1_, bf16[128,768]{1,0:T(8,128)(2,1)S(1)} %collective-permute-done.1.refs_2_, f32[64,128]{1,0:T(8,128)S(1)} %bitcast.15, bf16[768,2432]{1,0:T(8,128)(2,1)S(1)} %collective-permute-done.2.refs_4_, ...), custom_call_target="tpu_custom_call" | custom-call | tf_op jit(solution)/shard_map/output/pallas_call | solution.py:319
  22.2 0.5 collective-permute-start.3
  22.7 0.9 %collective-permute-done.3.refs_2_ = f32[64,128]{1,0:T(8,128)S(1)} collective-permute-done((f32[64,128]{1,0:T(8,128)S(1)}, f32[64,128]{1,0:T(8,128)S(1)}, u32[]{:S(2)}, u32[]{:S(2)}) %collective-permute-start.3) | collective-permute-done | bytes 32800 | tf_op jit(solution)/shard_map/ppermute | solution.py:381
  23.6 2.7 %theirs.3 = (bf16[256,2304]{1,0:T(8,128)(2,1)S(1)}, bf16[128,768]{1,0:T(8,128)(2,1)S(1)}) custom-call(s32[1]{0:T(128)S(6)} %copy.12.text_len.refs_0_, f32[64,128]{1,0:T(8,128)S(1)} %output.2.refs_1_.refs_2_.refs_3_, f32[64,128]{1,0:T(8,128)S(1)} %collective-permute-done.3.refs_2_, bf16[144,2432]{1,0:T(8,128)(2,1)S(1)} %get-tuple-element.15.refs_3_, ...), custom_call_target="tpu_custom_call" | custom-call | tf_op jit(solution)/shard_map/theirs/pallas_call | solution.py:319
  26.3 0.4 collective-permute-start.4
  26.7 2.1 %mine.3.refs_1_ = f32[128,2432]{1,0:T(8,128)S(1)} custom-call(s32[1]{0:T(128)S(6)} %copy.12.text_len.refs_0_, bf16[256,2304]{1,0:T(8,128)(2,1)S(1)} %get-tuple-element.23.refs_1_, f32[64,128]{1,0:T(8,128)S(1)} %output.2.refs_1_.refs_2_.refs_3_, bf16[144,2432]{1,0:T(8,128)(2,1)S(1)} %get-tuple-element.15.refs_3_, ...), custom_call_target="tpu_custom_call" | custom-call | tf_op jit(solution)/shard_map/mine/pallas_call | solution.py:319
  28.8 2.1 %output.3 = f32[64,128]{1,0:T(8,128)S(1)} custom-call(s32[1,3]{1,0:T(1,128)S(1)} %copy-done.3, f32[128,2432]{1,0:T(8,128)S(1)} %mine.3.refs_1_, bf16[128,768]{1,0:T(8,128)(2,1)S(1)} %collective-permute-done.4.refs_2_, f32[64,128]{1,0:T(8,128)S(1)} %output.2.refs_1_.refs_2_.refs_3_, bf16[768,2432]{1,0:T(8,128)(2,1)S(1)} %collective-permute-done.2.refs_4_, ...), custom_call_target="tpu_custom_call" | custom-call | tf_op jit(solution)/shard_map/output/pallas_call | solution.py:319
  31.0 3.1 %collective-permute-start.5 = (f32[64,128]{1,0:T(8,128)S(1)}, f32[64,128]{1,0:T(8,128)S(1)}, u32[]{:S(2)}, u32[]{:S(2)}) collective-permute-start(f32[64,128]{1,0:T(8,128)S(1)} %output.3), channel_id=1, source_target_pairs={{0,4},{2,6},{4,0},{6,2},{8,12},{10,14},{12,8},{14,10},{16,20},{18,... | collective-permute-start | bytes 98312 | tf_op jit(solution)/shard_map/ppermute | solution.py:287
  34.1 1.1 %collective-permute-start.6 = (f32[64,128]{1,0:T(8,128)S(1)}, f32[64,128]{1,0:T(8,128)S(1)}, u32[]{:S(2)}, u32[]{:S(2)}) collective-permute-start(f32[64,128]{1,0:T(8,128)S(1)} %output.3), channel_id=1, source_target_pairs={{0,6},{2,4},{4,2},{6,0},{8,14},{10,12},{12,10},{14,8},{16,22},{18,... | collective-permute-start | bytes 98312 | tf_op jit(solution)/shard_map/ppermute | solution.py:287
  35.2 1.2 %collective-permute-done.5 = f32[64,128]{1,0:T(8,128)S(1)} collective-permute-done((f32[64,128]{1,0:T(8,128)S(1)}, f32[64,128]{1,0:T(8,128)S(1)}, u32[]{:S(2)}, u32[]{:S(2)}) %collective-permute-start.5) | collective-permute-done | bytes 32800 | tf_op jit(solution)/shard_map/ppermute | solution.py:287
  36.5 2.7 %collective-permute-done.6 = f32[64,128]{1,0:T(8,128)S(1)} collective-permute-done((f32[64,128]{1,0:T(8,128)S(1)}, f32[64,128]{1,0:T(8,128)S(1)}, u32[]{:S(2)}, u32[]{:S(2)}) %collective-permute-start.6) | collective-permute-done | bytes 32800 | tf_op jit(solution)/shard_map/ppermute | solution.py:287
  39.2 1.7 %collective-permute-start.10 = (f32[64,128]{1,0:T(8,128)S(1)}, f32[64,128]{1,0:T(8,128)S(1)}, u32[]{:S(2)}, u32[]{:S(2)}) collective-permute-start(f32[64,128]{1,0:T(8,128)S(1)} %add_add_fusion.2), channel_id=1, source_target_pairs={{0,8},{2,10},{4,12},{6,14},{8,0},{10,2},{12,4},{14,6},{16,24},{18,... | collective-permute-start | bytes 98312 | tf_op jit(solution)/shard_map/ppermute | solution.py:287
  40.9 2.9 %collective-permute-start.8 = (f32[64,128]{1,0:T(8,128)S(1)}, f32[64,128]{1,0:T(8,128)S(1)}, u32[]{:S(2)}, u32[]{:S(2)}) collective-permute-start(f32[64,128]{1,0:T(8,128)S(1)} %add_add_fusion.2), channel_id=1, source_target_pairs={{0,16},{2,18},{4,20},{6,22},{8,24},{10,26},{12,28},{14,30},{16,0},... | collective-permute-start | bytes 98312 | tf_op jit(solution)/shard_map/ppermute | solution.py:287
  43.8 0.2 collective-permute-start.9
  44.0 2.4 %collective-permute-done.8 = f32[64,128]{1,0:T(8,128)S(1)} collective-permute-done((f32[64,128]{1,0:T(8,128)S(1)}, f32[64,128]{1,0:T(8,128)S(1)}, u32[]{:S(2)}, u32[]{:S(2)}) %collective-permute-start.8) | collective-permute-done | bytes 32800 | tf_op jit(solution)/shard_map/ppermute | solution.py:287
  46.4 2.5 %collective-permute-done.9 = f32[64,128]{1,0:T(8,128)S(1)} collective-permute-done((f32[64,128]{1,0:T(8,128)S(1)}, f32[64,128]{1,0:T(8,128)S(1)}, u32[]{:S(2)}, u32[]{:S(2)}) %collective-permute-start.9) | collective-permute-done | bytes 32800 | tf_op jit(solution)/shard_map/ppermute | solution.py:287
  48.9 3.4 %collective-permute-start.11 = (f32[64,128]{1,0:T(8,128)S(1)}, f32[64,128]{1,0:T(8,128)S(1)}, u32[]{:S(2)}, u32[]{:S(2)}) collective-permute-start(f32[64,128]{1,0:T(8,128)S(1)} %add_add_fusion.1), channel_id=1, source_target_pairs={{0,64},{2,66},{4,68},{6,70},{8,72},{10,74},{12,76},{14,78},{16,80}... | collective-permute-start | bytes 98312 | tf_op jit(solution)/shard_map/ppermute | solution.py:287
  52.3 1.6 %collective-permute-start.13 = (f32[64,128]{1,0:T(8,128)S(1)}, f32[64,128]{1,0:T(8,128)S(1)}, u32[]{:S(2)}, u32[]{:S(2)}) collective-permute-start(f32[64,128]{1,0:T(8,128)S(1)} %add_add_fusion.1), channel_id=1, source_target_pairs={{0,32},{2,34},{4,36},{6,38},{8,40},{10,42},{12,44},{14,46},{16,48}... | collective-permute-start | bytes 98312 | tf_op jit(solution)/shard_map/ppermute | solution.py:287
  53.8 0.3 collective-permute-done.11
  54.2 2.0 %collective-permute-done.12 = f32[64,128]{1,0:T(8,128)S(1)} collective-permute-done((f32[64,128]{1,0:T(8,128)S(1)}, f32[64,128]{1,0:T(8,128)S(1)}, u32[]{:S(2)}, u32[]{:S(2)}) %collective-permute-start.12) | collective-permute-done | bytes 32800 | tf_op jit(solution)/shard_map/ppermute | solution.py:287
  56.2 5.4 %collective-permute-start.14 = (f32[64,128]{1,0:T(8,128)S(1)}, f32[64,128]{1,0:T(8,128)S(1)}, u32[]{:S(2)}, u32[]{:S(2)}) collective-permute-start(f32[64,128]{1,0:T(8,128)S(1)} %add_add_fusion), channel_id=1, source_target_pairs={{0,224},{2,226},{4,228},{6,230},{8,232},{10,234},{12,236},{14,238}... | collective-permute-start | bytes 98312 | tf_op jit(solution)/shard_map/ppermute | solution.py:287
  61.6 0.6 slice.3
  62.8 0.7 %collective-permute-done.14 = f32[64,128]{1,0:T(8,128)S(1)} collective-permute-done((f32[64,128]{1,0:T(8,128)S(1)}, f32[64,128]{1,0:T(8,128)S(1)}, u32[]{:S(2)}, u32[]{:S(2)}) %collective-permute-start.14) | collective-permute-done | bytes 32800 | tf_op jit(solution)/shard_map/ppermute | solution.py:287
  63.5 0.6 %multiply_bitcast_fusion = f32[1,128,64]{1,2,0:T(8,128)} fusion(f32[64,128]{1,0:T(8,128)S(1)} %collective-permute-done.14, f32[64,128]{1,0:T(8,128)S(1)} %collective-permute-done.13, f32[64,128]{1,0:T(8,128)S(1)} %collective-permute-done.12, f32[64,128]{1,0:T(8,128)S(1)} %collective-permute-done.11, f32[64,128]{1,0:T(8,128)S(1)} %collective-permute-done.10, ...), kind=kLoop, calls=%fused_computation | loop fusion | flops 172032 | bytes 393230 | tf_op jit(solution)/shard_map/broadcast_in_dim | solution.py:383
  (18 shorter events, 0.1 us)
Async XLA Ops:
  0.0 20.0 %collective-permute-start.2 = (bf16[768,2432]{1,0:T(8,128)(2,1)}, bf16[768,2432]{1,0:T(8,128)(2,1)S(1)}, u32[]{:S(2)}, u32[]{:S(2)}) collective-permute-start(bf16[768,2432]{1,0:T(8,128)(2,1)} %refs_6_.3), channel_id=1, source_target_pairs={{0,1},{1,0},{2,3},{3,2},{4,5},{5,4},{6,7},{7,6},{8,9},{9,8},{10,11... | collective-permute-start | bytes 11206664 | tf_op jit(solution)/shard_map/ppermute | solution.py:314
  0.0 14.9 %collective-permute-start = (f32[64,128]{1,0:T(8,128)}, f32[64,128]{1,0:T(8,128)S(1)}, u32[]{:S(2)}, u32[]{:S(2)}) collective-permute-start(f32[64,128]{1,0:T(8,128)} %bitcast.12), channel_id=1, source_target_pairs={{0,1},{1,0},{2,3},{3,2},{4,5},{5,4},{6,7},{7,6},{8,9},{9,8},{10,11... | collective-permute-start | bytes 98312 | tf_op jit(solution)/shard_map/ppermute | solution.py:313
  1.2 13.7 %copy-start.2 = (f32[1,128,64]{1,2,0:T(8,128)S(1)}, f32[1,128,64]{1,2,0:T(8,128)}, u32[]{:S(2)}) copy-start(f32[1,128,64]{1,2,0:T(8,128)} %param.11) | copy-start | bytes 98308
  1.2 16.7 %copy-start = (bf16[768,2432]{1,0:T(8,128)(2,1)S(1)}, bf16[768,2432]{1,0:T(8,128)(2,1)}, u32[]{:S(2)}) copy-start(bf16[768,2432]{1,0:T(8,128)(2,1)} %refs_6_.3) | copy-start | bytes 11206660
  17.6 2.4 %collective-permute-start.1 = (bf16[128,768]{1,0:T(8,128)(2,1)S(1)}, bf16[128,768]{1,0:T(8,128)(2,1)S(1)}, u32[]{:S(2)}, u32[]{:S(2)}) collective-permute-start(bf16[128,768]{1,0:T(8,128)(2,1)S(1)} %get-tuple-element.20), channel_id=1, source_target_pairs={{0,1},{1,0},{2,3},{3,2},{4,5},{5,4},{6,7},{7,6},{8,9},{9,8},{10,11... | collective-permute-start | bytes 589832 | tf_op jit(solution)/shard_map/ppermute | solution.py:359
  17.9 2.1 %copy-start.1 = (bf16[2432,64]{0,1:T(8,128)(2,1)S(1)}, bf16[2432,64]{0,1:T(8,128)(2,1)}, u32[]{:S(2)}) copy-start(bf16[2432,64]{0,1:T(8,128)(2,1)} %param.20) | copy-start | bytes 933892
  17.9 2.1 %copy-start.3 = (s32[1,3]{1,0:T(1,128)S(1)}, s32[1,3]{1,0:T(1,128)}, u32[]{:S(2)}) copy-start(s32[1,3]{1,0:T(1,128)} %refs_0_.7) | copy-start | bytes 40
  22.2 1.4 %collective-permute-start.3 = (f32[64,128]{1,0:T(8,128)S(1)}, f32[64,128]{1,0:T(8,128)S(1)}, u32[]{:S(2)}, u32[]{:S(2)}) collective-permute-start(f32[64,128]{1,0:T(8,128)S(1)} %output.2.refs_1_.refs_2_.refs_3_), channel_id=1, source_target_pairs={{0,1},{1,0},{2,3},{3,2},{4,5},{5,4},{6,7},{7,6},{8,9},{9,8},{10,11... | collective-permute-start | bytes 98312 | tf_op jit(solution)/shard_map/ppermute | solution.py:381
  26.3 2.5 %collective-permute-start.4 = (bf16[128,768]{1,0:T(8,128)(2,1)S(1)}, bf16[128,768]{1,0:T(8,128)(2,1)S(1)}, u32[]{:S(2)}, u32[]{:S(2)}) collective-permute-start(bf16[128,768]{1,0:T(8,128)(2,1)S(1)} %get-tuple-element.24), channel_id=1, source_target_pairs={{0,1},{1,0},{2,3},{3,2},{4,5},{5,4},{6,7},{7,6},{8,9},{9,8},{10,11... | collective-permute-start | bytes 589832 | tf_op jit(solution)/shard_map/ppermute | solution.py:359
  31.0 5.5 %collective-permute-start.5 = (f32[64,128]{1,0:T(8,128)S(1)}, f32[64,128]{1,0:T(8,128)S(1)}, u32[]{:S(2)}, u32[]{:S(2)}) collective-permute-start(f32[64,128]{1,0:T(8,128)S(1)} %output.3), channel_id=1, source_target_pairs={{0,4},{2,6},{4,0},{6,2},{8,12},{10,14},{12,8},{14,10},{16,20},{18,... | collective-permute-start | bytes 98312 | tf_op jit(solution)/shard_map/ppermute | solution.py:287
  34.1 5.1 %collective-permute-start.6 = (f32[64,128]{1,0:T(8,128)S(1)}, f32[64,128]{1,0:T(8,128)S(1)}, u32[]{:S(2)}, u32[]{:S(2)}) collective-permute-start(f32[64,128]{1,0:T(8,128)S(1)} %output.3), channel_id=1, source_target_pairs={{0,6},{2,4},{4,2},{6,0},{8,14},{10,12},{12,10},{14,8},{16,22},{18,... | collective-permute-start | bytes 98312 | tf_op jit(solution)/shard_map/ppermute | solution.py:287
  35.2 4.0 %collective-permute-start.7 = (f32[64,128]{1,0:T(8,128)S(1)}, f32[64,128]{1,0:T(8,128)S(1)}, u32[]{:S(2)}, u32[]{:S(2)}) collective-permute-start(f32[64,128]{1,0:T(8,128)S(1)} %output.3), channel_id=1, source_target_pairs={{0,2},{2,0},{4,6},{6,4},{8,10},{10,8},{12,14},{14,12},{16,18},{18,... | collective-permute-start | bytes 98312 | tf_op jit(solution)/shard_map/ppermute | solution.py:287
  39.2 4.8 %collective-permute-start.10 = (f32[64,128]{1,0:T(8,128)S(1)}, f32[64,128]{1,0:T(8,128)S(1)}, u32[]{:S(2)}, u32[]{:S(2)}) collective-permute-start(f32[64,128]{1,0:T(8,128)S(1)} %add_add_fusion.2), channel_id=1, source_target_pairs={{0,8},{2,10},{4,12},{6,14},{8,0},{10,2},{12,4},{14,6},{16,24},{18,... | collective-permute-start | bytes 98312 | tf_op jit(solution)/shard_map/ppermute | solution.py:287
  40.9 5.5 %collective-permute-start.8 = (f32[64,128]{1,0:T(8,128)S(1)}, f32[64,128]{1,0:T(8,128)S(1)}, u32[]{:S(2)}, u32[]{:S(2)}) collective-permute-start(f32[64,128]{1,0:T(8,128)S(1)} %add_add_fusion.2), channel_id=1, source_target_pairs={{0,16},{2,18},{4,20},{6,22},{8,24},{10,26},{12,28},{14,30},{16,0},... | collective-permute-start | bytes 98312 | tf_op jit(solution)/shard_map/ppermute | solution.py:287
  43.8 5.1 %collective-permute-start.9 = (f32[64,128]{1,0:T(8,128)S(1)}, f32[64,128]{1,0:T(8,128)S(1)}, u32[]{:S(2)}, u32[]{:S(2)}) collective-permute-start(f32[64,128]{1,0:T(8,128)S(1)} %add_add_fusion.2), channel_id=1, source_target_pairs={{0,24},{2,26},{4,28},{6,30},{8,16},{10,18},{12,20},{14,22},{16,8},... | collective-permute-start | bytes 98312 | tf_op jit(solution)/shard_map/ppermute | solution.py:287
  48.9 5.2 %collective-permute-start.11 = (f32[64,128]{1,0:T(8,128)S(1)}, f32[64,128]{1,0:T(8,128)S(1)}, u32[]{:S(2)}, u32[]{:S(2)}) collective-permute-start(f32[64,128]{1,0:T(8,128)S(1)} %add_add_fusion.1), channel_id=1, source_target_pairs={{0,64},{2,66},{4,68},{6,70},{8,72},{10,74},{12,76},{14,78},{16,80}... | collective-permute-start | bytes 98312 | tf_op jit(solution)/shard_map/ppermute | solution.py:287
  52.3 3.9 %collective-permute-start.12 = (f32[64,128]{1,0:T(8,128)S(1)}, f32[64,128]{1,0:T(8,128)S(1)}, u32[]{:S(2)}, u32[]{:S(2)}) collective-permute-start(f32[64,128]{1,0:T(8,128)S(1)} %add_add_fusion.1), channel_id=1, source_target_pairs={{0,96},{2,98},{4,100},{6,102},{8,104},{10,106},{12,108},{14,110},{... | collective-permute-start | bytes 98312 | tf_op jit(solution)/shard_map/ppermute | solution.py:287
  52.3 3.9 %collective-permute-start.13 = (f32[64,128]{1,0:T(8,128)S(1)}, f32[64,128]{1,0:T(8,128)S(1)}, u32[]{:S(2)}, u32[]{:S(2)}) collective-permute-start(f32[64,128]{1,0:T(8,128)S(1)} %add_add_fusion.1), channel_id=1, source_target_pairs={{0,32},{2,34},{4,36},{6,38},{8,40},{10,42},{12,44},{14,46},{16,48}... | collective-permute-start | bytes 98312 | tf_op jit(solution)/shard_map/ppermute | solution.py:287
  56.2 7.3 %collective-permute-start.14 = (f32[64,128]{1,0:T(8,128)S(1)}, f32[64,128]{1,0:T(8,128)S(1)}, u32[]{:S(2)}, u32[]{:S(2)}) collective-permute-start(f32[64,128]{1,0:T(8,128)S(1)} %add_add_fusion), channel_id=1, source_target_pairs={{0,224},{2,226},{4,228},{6,230},{8,232},{10,234},{12,236},{14,238}... | collective-permute-start | bytes 98312 | tf_op jit(solution)/shard_map/ppermute | solution.py:287

commit v4 on v3

--- a/solution.py
+++ b/solution.py
@@ -255,10 +255,21 @@
 
 def output_kernel(t, steps, residual, came, latent, proj_other, embed_out, *rest):
     result = rest[-1]
-    whole = residual[...] + dot(came[...], proj_other[...])
-    mean, scale = row_stats(whole)
-    normed = ((whole - mean) * scale).astype(BF16)
-    velocity = dot_t(embed_out[...], normed)
+    model = residual.shape[1]
+    cuts = [slice(low, min(low + 2 * CHUNK, model)) for low in range(0, model, 2 * CHUNK)]
+    parts, total = [], 0.0
+    out = dot(came[...], proj_other[:, cuts[0]])
+    for k, cut in enumerate(cuts):
+        later = dot(came[...], proj_other[:, cuts[k + 1]]) if k + 1 < len(cuts) else None
+        parts.append(residual[:, cut] + out)
+        total = total + jnp.sum(parts[-1], -1, keepdims=True)
+        out = later
+    mean = total / model
+    spread = sum(jnp.sum((part - mean) * (part - mean), -1, keepdims=True) for part in parts)
+    scale = lax.rsqrt(spread / model + epsilon)
+    velocity = 0.0
+    for cut, part in zip(cuts, parts):
+        velocity = velocity + dot_t(embed_out[:, cut], ((part - mean) * scale).astype(BF16))
     a, m, b = (steps[0, k].astype(F32) / 1000.0 for k in range(3))
     if t == 0:
         result[...] = latent[...] + (m - a) * velocity

time: 64.4 us -> 64.2 us (level)
  no operation moved by 1% of the time
where the time goes in v4:
time: 64.2 us; the launch traced here: 63.9 us
  Pallas kernels  27.3 us (43%)
  starting transfers between devices  21.1 us (33%)
  waiting for transfers between devices  12.8 us (20%)
  between operations  1.47 us (2%)
  other arithmetic  0.68 us (1%)
    pallas_call x7, Pallas kernels, call(): pl.pallas_call(kernel, out_shape=[pltpu.VMEM(dims, dtype) for dims, dtype...  27.3 us
    ppermute x10, starting transfers between devices, prefix_sum(): came.append((flip, lax.ppermute(total, axis, pairs)))  19.3 us
    ppermute x10, waiting for transfers between devices, prefix_sum(): came.append((flip, lax.ppermute(total, axis, pairs)))  11.9 us
  transfers between devices with their start and end apart: 15, of which 8 were waited for; matrix products, arithmetic and copies ran while one was open for 1% of the time, Pallas kernels for 32%

profile of v4, /device:TPU:32, one launch (start us, length us, event | category | flops | bytes accessed | tf_op | source)
XLA Modules:
  0.0 63.9 jit_solution(17889151660757244579)
XLA Ops:
  0.0 0.0 collective-permute-start.2
  0.0 0.5 collective-permute-start
  1.2 13.7 %prepare.1 = (bf16[144,2432]{1,0:T(8,128)(2,1)S(1)}, bf16[144,2304]{1,0:T(8,128)(2,1)S(1)}, bf16[384,768]{1,0:T(8,128)(2,1)S(1)}, bf16[384,768]{1,0:T(8,128)(2,1...) custom-call(s32[1,3]{1,0:T(1,128)} %refs_0_.7, s32[1]{0:T(128)S(6)} %copy.12.text_len.refs_0_, ...), custom_call_target="tpu_custom_call" | custom-call | tf_op jit(solution)/shard_map/prepare/pallas_call | solution.py:330
  14.9 2.7 %theirs.2 = (bf16[256,2304]{1,0:T(8,128)(2,1)S(1)}, bf16[128,768]{1,0:T(8,128)(2,1)S(1)}) custom-call(s32[1]{0:T(128)S(6)} %copy.12.text_len.refs_0_, f32[64,128]{1,0:T(8,128)S(1)} %bitcast.13, f32[64,128]{1,0:T(8,128)S(1)} %collective-permute-done.refs_2_, bf16[144,2432]{1,0:T(8,128)(2,1)S(1)} %get-tuple-element.15.refs_3_, ...), custom_call_target="tpu_custom_call" | custom-call | tf_op jit(solution)/shard_map/theirs/pallas_call | solution.py:330
  17.6 0.3 collective-permute-start.1
  17.9 0.0 copy-start.1
  17.9 0.0 copy-start.3
  17.9 2.1 %mine.2.refs_1_ = f32[128,2432]{1,0:T(8,128)S(1)} custom-call(s32[1]{0:T(128)S(6)} %copy.12.text_len.refs_0_, bf16[256,2304]{1,0:T(8,128)(2,1)S(1)} %get-tuple-element.19.refs_1_, f32[64,128]{1,0:T(8,128)S(1)} %bitcast.14, bf16[144,2432]{1,0:T(8,128)(2,1)S(1)} %get-tuple-element.15.refs_3_, bf16[384,768]{1,0:T(8,128)(2,1)S(1)} %get-tuple-element.17.refs_5_.refs_4_, ...), custom_call_target="tpu_custom_call" | custom-call | tf_op jit(solution)/shard_map/mine/pallas_call | solution.py:330
  20.1 2.0 %output.2.refs_1_.refs_2_.refs_3_ = f32[64,128]{1,0:T(8,128)S(1)} custom-call(s32[1,3]{1,0:T(1,128)S(1)} %copy-done.3, f32[128,2432]{1,0:T(8,128)S(1)} %mine.2.refs_1_, bf16[128,768]{1,0:T(8,128)(2,1)S(1)} %collective-permute-done.1.refs_2_, f32[64,128]{1,0:T(8,128)S(1)} %bitcast.15, bf16[768,2432]{1,0:T(8,128)(2,1)S(1)} %collective-permute-done.2.refs_4_, ...), custom_call_target="tpu_custom_call" | custom-call | tf_op jit(solution)/shard_map/output/pallas_call | solution.py:330
  22.1 0.6 collective-permute-start.3
  22.7 0.9 %collective-permute-done.3.refs_2_ = f32[64,128]{1,0:T(8,128)S(1)} collective-permute-done((f32[64,128]{1,0:T(8,128)S(1)}, f32[64,128]{1,0:T(8,128)S(1)}, u32[]{:S(2)}, u32[]{:S(2)}) %collective-permute-start.3) | collective-permute-done | bytes 32800 | tf_op jit(solution)/shard_map/ppermute | solution.py:392
  23.5 2.7 %theirs.3 = (bf16[256,2304]{1,0:T(8,128)(2,1)S(1)}, bf16[128,768]{1,0:T(8,128)(2,1)S(1)}) custom-call(s32[1]{0:T(128)S(6)} %copy.12.text_len.refs_0_, f32[64,128]{1,0:T(8,128)S(1)} %output.2.refs_1_.refs_2_.refs_3_, f32[64,128]{1,0:T(8,128)S(1)} %collective-permute-done.3.refs_2_, bf16[144,2432]{1,0:T(8,128)(2,1)S(1)} %get-tuple-element.15.refs_3_, ...), custom_call_target="tpu_custom_call" | custom-call | tf_op jit(solution)/shard_map/theirs/pallas_call | solution.py:330
  26.2 0.4 collective-permute-start.4
  26.6 2.1 %mine.3.refs_1_ = f32[128,2432]{1,0:T(8,128)S(1)} custom-call(s32[1]{0:T(128)S(6)} %copy.12.text_len.refs_0_, bf16[256,2304]{1,0:T(8,128)(2,1)S(1)} %get-tuple-element.23.refs_1_, f32[64,128]{1,0:T(8,128)S(1)} %output.2.refs_1_.refs_2_.refs_3_, bf16[144,2432]{1,0:T(8,128)(2,1)S(1)} %get-tuple-element.15.refs_3_, ...), custom_call_target="tpu_custom_call" | custom-call | tf_op jit(solution)/shard_map/mine/pallas_call | solution.py:330
  28.7 2.0 %output.3 = f32[64,128]{1,0:T(8,128)S(1)} custom-call(s32[1,3]{1,0:T(1,128)S(1)} %copy-done.3, f32[128,2432]{1,0:T(8,128)S(1)} %mine.3.refs_1_, bf16[128,768]{1,0:T(8,128)(2,1)S(1)} %collective-permute-done.4.refs_2_, f32[64,128]{1,0:T(8,128)S(1)} %output.2.refs_1_.refs_2_.refs_3_, bf16[768,2432]{1,0:T(8,128)(2,1)S(1)} %collective-permute-done.2.refs_4_, ...), custom_call_target="tpu_custom_call" | custom-call | tf_op jit(solution)/shard_map/output/pallas_call | solution.py:330
  30.8 3.1 %collective-permute-start.5 = (f32[64,128]{1,0:T(8,128)S(1)}, f32[64,128]{1,0:T(8,128)S(1)}, u32[]{:S(2)}, u32[]{:S(2)}) collective-permute-start(f32[64,128]{1,0:T(8,128)S(1)} %output.3), channel_id=1, source_target_pairs={{0,4},{2,6},{4,0},{6,2},{8,12},{10,14},{12,8},{14,10},{16,20},{18,... | collective-permute-start | bytes 98312 | tf_op jit(solution)/shard_map/ppermute | solution.py:298
  33.9 1.1 %collective-permute-start.6 = (f32[64,128]{1,0:T(8,128)S(1)}, f32[64,128]{1,0:T(8,128)S(1)}, u32[]{:S(2)}, u32[]{:S(2)}) collective-permute-start(f32[64,128]{1,0:T(8,128)S(1)} %output.3), channel_id=1, source_target_pairs={{0,6},{2,4},{4,2},{6,0},{8,14},{10,12},{12,10},{14,8},{16,22},{18,... | collective-permute-start | bytes 98312 | tf_op jit(solution)/shard_map/ppermute | solution.py:298
  35.0 1.2 %collective-permute-done.5 = f32[64,128]{1,0:T(8,128)S(1)} collective-permute-done((f32[64,128]{1,0:T(8,128)S(1)}, f32[64,128]{1,0:T(8,128)S(1)}, u32[]{:S(2)}, u32[]{:S(2)}) %collective-permute-start.5) | collective-permute-done | bytes 32800 | tf_op jit(solution)/shard_map/ppermute | solution.py:298
  36.3 2.7 %collective-permute-done.6 = f32[64,128]{1,0:T(8,128)S(1)} collective-permute-done((f32[64,128]{1,0:T(8,128)S(1)}, f32[64,128]{1,0:T(8,128)S(1)}, u32[]{:S(2)}, u32[]{:S(2)}) %collective-permute-start.6) | collective-permute-done | bytes 32800 | tf_op jit(solution)/shard_map/ppermute | solution.py:298
  39.0 1.7 %collective-permute-start.10 = (f32[64,128]{1,0:T(8,128)S(1)}, f32[64,128]{1,0:T(8,128)S(1)}, u32[]{:S(2)}, u32[]{:S(2)}) collective-permute-start(f32[64,128]{1,0:T(8,128)S(1)} %add_add_fusion.2), channel_id=1, source_target_pairs={{0,8},{2,10},{4,12},{6,14},{8,0},{10,2},{12,4},{14,6},{16,24},{18,... | collective-permute-start | bytes 98312 | tf_op jit(solution)/shard_map/ppermute | solution.py:298
  40.7 2.9 %collective-permute-start.8 = (f32[64,128]{1,0:T(8,128)S(1)}, f32[64,128]{1,0:T(8,128)S(1)}, u32[]{:S(2)}, u32[]{:S(2)}) collective-permute-start(f32[64,128]{1,0:T(8,128)S(1)} %add_add_fusion.2), channel_id=1, source_target_pairs={{0,16},{2,18},{4,20},{6,22},{8,24},{10,26},{12,28},{14,30},{16,0},... | collective-permute-start | bytes 98312 | tf_op jit(solution)/shard_map/ppermute | solution.py:298
  43.6 0.2 collective-permute-start.9
  43.8 2.4 %collective-permute-done.8 = f32[64,128]{1,0:T(8,128)S(1)} collective-permute-done((f32[64,128]{1,0:T(8,128)S(1)}, f32[64,128]{1,0:T(8,128)S(1)}, u32[]{:S(2)}, u32[]{:S(2)}) %collective-permute-start.8) | collective-permute-done | bytes 32800 | tf_op jit(solution)/shard_map/ppermute | solution.py:298
  46.2 2.5 %collective-permute-done.9 = f32[64,128]{1,0:T(8,128)S(1)} collective-permute-done((f32[64,128]{1,0:T(8,128)S(1)}, f32[64,128]{1,0:T(8,128)S(1)}, u32[]{:S(2)}, u32[]{:S(2)}) %collective-permute-start.9) | collective-permute-done | bytes 32800 | tf_op jit(solution)/shard_map/ppermute | solution.py:298
  48.7 3.4 %collective-permute-start.11 = (f32[64,128]{1,0:T(8,128)S(1)}, f32[64,128]{1,0:T(8,128)S(1)}, u32[]{:S(2)}, u32[]{:S(2)}) collective-permute-start(f32[64,128]{1,0:T(8,128)S(1)} %add_add_fusion.1), channel_id=1, source_target_pairs={{0,64},{2,66},{4,68},{6,70},{8,72},{10,74},{12,76},{14,78},{16,80}... | collective-permute-start | bytes 98312 | tf_op jit(solution)/shard_map/ppermute | solution.py:298
  52.1 1.6 %collective-permute-start.13 = (f32[64,128]{1,0:T(8,128)S(1)}, f32[64,128]{1,0:T(8,128)S(1)}, u32[]{:S(2)}, u32[]{:S(2)}) collective-permute-start(f32[64,128]{1,0:T(8,128)S(1)} %add_add_fusion.1), channel_id=1, source_target_pairs={{0,32},{2,34},{4,36},{6,38},{8,40},{10,42},{12,44},{14,46},{16,48}... | collective-permute-start | bytes 98312 | tf_op jit(solution)/shard_map/ppermute | solution.py:298
  53.6 0.3 collective-permute-done.11
  54.0 2.0 %collective-permute-done.12 = f32[64,128]{1,0:T(8,128)S(1)} collective-permute-done((f32[64,128]{1,0:T(8,128)S(1)}, f32[64,128]{1,0:T(8,128)S(1)}, u32[]{:S(2)}, u32[]{:S(2)}) %collective-permute-start.12) | collective-permute-done | bytes 32800 | tf_op jit(solution)/shard_map/ppermute | solution.py:298
  56.0 5.4 %collective-permute-start.14 = (f32[64,128]{1,0:T(8,128)S(1)}, f32[64,128]{1,0:T(8,128)S(1)}, u32[]{:S(2)}, u32[]{:S(2)}) collective-permute-start(f32[64,128]{1,0:T(8,128)S(1)} %add_add_fusion), channel_id=1, source_target_pairs={{0,224},{2,226},{4,228},{6,230},{8,232},{10,234},{12,236},{14,238}... | collective-permute-start | bytes 98312 | tf_op jit(solution)/shard_map/ppermute | solution.py:298
  61.4 0.6 slice.3
  62.6 0.7 %collective-permute-done.14 = f32[64,128]{1,0:T(8,128)S(1)} collective-permute-done((f32[64,128]{1,0:T(8,128)S(1)}, f32[64,128]{1,0:T(8,128)S(1)}, u32[]{:S(2)}, u32[]{:S(2)}) %collective-permute-start.14) | collective-permute-done | bytes 32800 | tf_op jit(solution)/shard_map/ppermute | solution.py:298
  63.3 0.6 %multiply_bitcast_fusion = f32[1,128,64]{1,2,0:T(8,128)} fusion(f32[64,128]{1,0:T(8,128)S(1)} %collective-permute-done.14, f32[64,128]{1,0:T(8,128)S(1)} %collective-permute-done.13, f32[64,128]{1,0:T(8,128)S(1)} %collective-permute-done.12, f32[64,128]{1,0:T(8,128)S(1)} %collective-permute-done.11, f32[64,128]{1,0:T(8,128)S(1)} %collective-permute-done.10, ...), kind=kLoop, calls=%fused_computation | loop fusion | flops 172032 | bytes 393230 | tf_op jit(solution)/shard_map/broadcast_in_dim | solution.py:394
  (18 shorter events, 0.1 us)
Async XLA Ops:
  0.0 20.0 %collective-permute-start.2 = (bf16[768,2432]{1,0:T(8,128)(2,1)}, bf16[768,2432]{1,0:T(8,128)(2,1)S(1)}, u32[]{:S(2)}, u32[]{:S(2)}) collective-permute-start(bf16[768,2432]{1,0:T(8,128)(2,1)} %refs_6_.3), channel_id=1, source_target_pairs={{0,1},{1,0},{2,3},{3,2},{4,5},{5,4},{6,7},{7,6},{8,9},{9,8},{10,11... | collective-permute-start | bytes 11206664 | tf_op jit(solution)/shard_map/ppermute | solution.py:325
  0.0 14.9 %collective-permute-start = (f32[64,128]{1,0:T(8,128)}, f32[64,128]{1,0:T(8,128)S(1)}, u32[]{:S(2)}, u32[]{:S(2)}) collective-permute-start(f32[64,128]{1,0:T(8,128)} %bitcast.12), channel_id=1, source_target_pairs={{0,1},{1,0},{2,3},{3,2},{4,5},{5,4},{6,7},{7,6},{8,9},{9,8},{10,11... | collective-permute-start | bytes 98312 | tf_op jit(solution)/shard_map/ppermute | solution.py:324
  1.2 13.7 %copy-start.2 = (f32[1,128,64]{1,2,0:T(8,128)S(1)}, f32[1,128,64]{1,2,0:T(8,128)}, u32[]{:S(2)}) copy-start(f32[1,128,64]{1,2,0:T(8,128)} %param.11) | copy-start | bytes 98308
  1.2 16.7 %copy-start = (bf16[768,2432]{1,0:T(8,128)(2,1)S(1)}, bf16[768,2432]{1,0:T(8,128)(2,1)}, u32[]{:S(2)}) copy-start(bf16[768,2432]{1,0:T(8,128)(2,1)} %refs_6_.3) | copy-start | bytes 11206660
  17.6 2.4 %collective-permute-start.1 = (bf16[128,768]{1,0:T(8,128)(2,1)S(1)}, bf16[128,768]{1,0:T(8,128)(2,1)S(1)}, u32[]{:S(2)}, u32[]{:S(2)}) collective-permute-start(bf16[128,768]{1,0:T(8,128)(2,1)S(1)} %get-tuple-element.20), channel_id=1, source_target_pairs={{0,1},{1,0},{2,3},{3,2},{4,5},{5,4},{6,7},{7,6},{8,9},{9,8},{10,11... | collective-permute-start | bytes 589832 | tf_op jit(solution)/shard_map/ppermute | solution.py:370
  17.9 2.1 %copy-start.1 = (bf16[2432,64]{0,1:T(8,128)(2,1)S(1)}, bf16[2432,64]{0,1:T(8,128)(2,1)}, u32[]{:S(2)}) copy-start(bf16[2432,64]{0,1:T(8,128)(2,1)} %param.20) | copy-start | bytes 933892
  17.9 2.1 %copy-start.3 = (s32[1,3]{1,0:T(1,128)S(1)}, s32[1,3]{1,0:T(1,128)}, u32[]{:S(2)}) copy-start(s32[1,3]{1,0:T(1,128)} %refs_0_.7) | copy-start | bytes 40
  22.1 1.4 %collective-permute-start.3 = (f32[64,128]{1,0:T(8,128)S(1)}, f32[64,128]{1,0:T(8,128)S(1)}, u32[]{:S(2)}, u32[]{:S(2)}) collective-permute-start(f32[64,128]{1,0:T(8,128)S(1)} %output.2.refs_1_.refs_2_.refs_3_), channel_id=1, source_target_pairs={{0,1},{1,0},{2,3},{3,2},{4,5},{5,4},{6,7},{7,6},{8,9},{9,8},{10,11... | collective-permute-start | bytes 98312 | tf_op jit(solution)/shard_map/ppermute | solution.py:392
  26.2 2.5 %collective-permute-start.4 = (bf16[128,768]{1,0:T(8,128)(2,1)S(1)}, bf16[128,768]{1,0:T(8,128)(2,1)S(1)}, u32[]{:S(2)}, u32[]{:S(2)}) collective-permute-start(bf16[128,768]{1,0:T(8,128)(2,1)S(1)} %get-tuple-element.24), channel_id=1, source_target_pairs={{0,1},{1,0},{2,3},{3,2},{4,5},{5,4},{6,7},{7,6},{8,9},{9,8},{10,11... | collective-permute-start | bytes 589832 | tf_op jit(solution)/shard_map/ppermute | solution.py:370
  30.8 5.5 %collective-permute-start.5 = (f32[64,128]{1,0:T(8,128)S(1)}, f32[64,128]{1,0:T(8,128)S(1)}, u32[]{:S(2)}, u32[]{:S(2)}) collective-permute-start(f32[64,128]{1,0:T(8,128)S(1)} %output.3), channel_id=1, source_target_pairs={{0,4},{2,6},{4,0},{6,2},{8,12},{10,14},{12,8},{14,10},{16,20},{18,... | collective-permute-start | bytes 98312 | tf_op jit(solution)/shard_map/ppermute | solution.py:298
  33.9 5.1 %collective-permute-start.6 = (f32[64,128]{1,0:T(8,128)S(1)}, f32[64,128]{1,0:T(8,128)S(1)}, u32[]{:S(2)}, u32[]{:S(2)}) collective-permute-start(f32[64,128]{1,0:T(8,128)S(1)} %output.3), channel_id=1, source_target_pairs={{0,6},{2,4},{4,2},{6,0},{8,14},{10,12},{12,10},{14,8},{16,22},{18,... | collective-permute-start | bytes 98312 | tf_op jit(solution)/shard_map/ppermute | solution.py:298
  35.0 4.0 %collective-permute-start.7 = (f32[64,128]{1,0:T(8,128)S(1)}, f32[64,128]{1,0:T(8,128)S(1)}, u32[]{:S(2)}, u32[]{:S(2)}) collective-permute-start(f32[64,128]{1,0:T(8,128)S(1)} %output.3), channel_id=1, source_target_pairs={{0,2},{2,0},{4,6},{6,4},{8,10},{10,8},{12,14},{14,12},{16,18},{18,... | collective-permute-start | bytes 98312 | tf_op jit(solution)/shard_map/ppermute | solution.py:298
  39.0 4.8 %collective-permute-start.10 = (f32[64,128]{1,0:T(8,128)S(1)}, f32[64,128]{1,0:T(8,128)S(1)}, u32[]{:S(2)}, u32[]{:S(2)}) collective-permute-start(f32[64,128]{1,0:T(8,128)S(1)} %add_add_fusion.2), channel_id=1, source_target_pairs={{0,8},{2,10},{4,12},{6,14},{8,0},{10,2},{12,4},{14,6},{16,24},{18,... | collective-permute-start | bytes 98312 | tf_op jit(solution)/shard_map/ppermute | solution.py:298
  40.7 5.5 %collective-permute-start.8 = (f32[64,128]{1,0:T(8,128)S(1)}, f32[64,128]{1,0:T(8,128)S(1)}, u32[]{:S(2)}, u32[]{:S(2)}) collective-permute-start(f32[64,128]{1,0:T(8,128)S(1)} %add_add_fusion.2), channel_id=1, source_target_pairs={{0,16},{2,18},{4,20},{6,22},{8,24},{10,26},{12,28},{14,30},{16,0},... | collective-permute-start | bytes 98312 | tf_op jit(solution)/shard_map/ppermute | solution.py:298
  43.6 5.1 %collective-permute-start.9 = (f32[64,128]{1,0:T(8,128)S(1)}, f32[64,128]{1,0:T(8,128)S(1)}, u32[]{:S(2)}, u32[]{:S(2)}) collective-permute-start(f32[64,128]{1,0:T(8,128)S(1)} %add_add_fusion.2), channel_id=1, source_target_pairs={{0,24},{2,26},{4,28},{6,30},{8,16},{10,18},{12,20},{14,22},{16,8},... | collective-permute-start | bytes 98312 | tf_op jit(solution)/shard_map/ppermute | solution.py:298
  48.7 5.3 %collective-permute-start.11 = (f32[64,128]{1,0:T(8,128)S(1)}, f32[64,128]{1,0:T(8,128)S(1)}, u32[]{:S(2)}, u32[]{:S(2)}) collective-permute-start(f32[64,128]{1,0:T(8,128)S(1)} %add_add_fusion.1), channel_id=1, source_target_pairs={{0,64},{2,66},{4,68},{6,70},{8,72},{10,74},{12,76},{14,78},{16,80}... | collective-permute-start | bytes 98312 | tf_op jit(solution)/shard_map/ppermute | solution.py:298
  52.1 3.9 %collective-permute-start.12 = (f32[64,128]{1,0:T(8,128)S(1)}, f32[64,128]{1,0:T(8,128)S(1)}, u32[]{:S(2)}, u32[]{:S(2)}) collective-permute-start(f32[64,128]{1,0:T(8,128)S(1)} %add_add_fusion.1), channel_id=1, source_target_pairs={{0,96},{2,98},{4,100},{6,102},{8,104},{10,106},{12,108},{14,110},{... | collective-permute-start | bytes 98312 | tf_op jit(solution)/shard_map/ppermute | solution.py:298
  52.1 3.9 %collective-permute-start.13 = (f32[64,128]{1,0:T(8,128)S(1)}, f32[64,128]{1,0:T(8,128)S(1)}, u32[]{:S(2)}, u32[]{:S(2)}) collective-permute-start(f32[64,128]{1,0:T(8,128)S(1)} %add_add_fusion.1), channel_id=1, source_target_pairs={{0,32},{2,34},{4,36},{6,38},{8,40},{10,42},{12,44},{14,46},{16,48}... | collective-permute-start | bytes 98312 | tf_op jit(solution)/shard_map/ppermute | solution.py:298
  56.0 7.3 %collective-permute-start.14 = (f32[64,128]{1,0:T(8,128)S(1)}, f32[64,128]{1,0:T(8,128)S(1)}, u32[]{:S(2)}, u32[]{:S(2)}) collective-permute-start(f32[64,128]{1,0:T(8,128)S(1)} %add_add_fusion), channel_id=1, source_target_pairs={{0,224},{2,226},{4,228},{6,230},{8,232},{10,234},{12,236},{14,238}... | collective-permute-start | bytes 98312 | tf_op jit(solution)/shard_map/ppermute | solution.py:298
